TPU v7x, 512 devices: a whole 4x8x8 slice. The times are simulated.
512 devices in a mesh: grp: 8 (over x, core), sp: 64 (over z, y).
Axes of the slice: x: 4, y: 8, z: 8, core: 2. Of those that a mesh axis runs over, the one named last changes fastest.
Arguments:
- upper_out: bfloat16 [65536, 2048], P(('grp', 'sp')), may hold values from -6 to 6
- lower_out: bfloat16 [65536, 2048], P(('grp', 'sp')), may hold values from -6 to 6
- upper_grad: bfloat16 [65536, 2048], P(('grp', 'sp')), may hold values from -6 to 6
- lower_grad: bfloat16 [65536, 2048], P(('grp', 'sp')), may hold values from -6 to 6
- norm_gain: float32 [2048], replicated, may hold values from 0.5 to 1.5
- query_weight: bfloat16 [2048, 1024], P('sp')
- key_weight: bfloat16 [2048, 256], P('sp')
- value_matrix: bfloat16 [2048, 256], P('sp'), may hold values from -0.125 to 0.125
- out_weight: bfloat16 [1024, 2048], P('sp'), may hold values from -0.1875 to 0.1875
- route_table: int32 [8, 64, 8], P('grp', 'sp'), may hold values from 0 to 7, each once within a row
- doc_lengths: int32 [8, 32], P('grp'), may hold values from 1 to 512, 8192 in all within a row
Outputs:
- restored: bfloat16 [65536, 2048], P(('grp', 'sp'))
- back_grad: bfloat16 [65536, 2048], P(('grp', 'sp'))
Inputs may be any that keep to these rules, and one draw needn't show every extreme that they name: `route_table`: each device's list of 8 destinations names every group once. `doc_lengths`: each group's 32 lengths sum to 8192; the longest is exactly 512.
All inputs are finite; a program needn't handle non-finite values.
Results may differ from a plain program's by a relative error of at most 0.015.
Values may be sent and summed in bfloat16 or wider, within the bound.
A program may use at most 64 MiB of HBM per device.

v0:
```python
import math

import jax
import jax.numpy as jnp
from jax import lax
from jax.sharding import PartitionSpec as P

HEAD_WIDTH = 64
LONGEST = 512


def attend(
    queries, out_grad, key_rows, value_rows, query_pos, doc_ids, block_rows, window, longest
):
    count = queries.shape[0]
    grand_total = key_rows.shape[0]
    head_size = queries.shape[1]
    scale = 1.0 / math.sqrt(head_size)
    blocks = count // block_rows

    def step(carry, index):
        key_acc, value_acc = carry
        first = index * block_rows
        q_block = lax.dynamic_slice_in_dim(queries, first, block_rows, 0)
        g_block = lax.dynamic_slice_in_dim(out_grad, first, block_rows, 0)
        p_block = lax.dynamic_slice_in_dim(query_pos, first, block_rows, 0)
        start = jnp.clip(p_block[0] - longest + 1, 0, grand_total - window)
        k_win = lax.dynamic_slice_in_dim(key_rows, start, window, 0)
        v_win = lax.dynamic_slice_in_dim(value_rows, start, window, 0)
        d_win = lax.dynamic_slice_in_dim(doc_ids, start, window, 0)
        k_pos = start + jnp.arange(window, dtype=jnp.int32)
        q_doc = jnp.take(doc_ids, p_block)
        allowed = (d_win[None, :] == q_doc[:, None]) & (k_pos[None, :] <= p_block[:, None])
        scores = jnp.dot(q_block, k_win.T, preferred_element_type=jnp.float32) * scale
        scores = jnp.where(allowed, scores, -jnp.inf)
        peak = jnp.max(scores, axis=1, keepdims=True)
        raised = jnp.exp(scores - peak)
        probs = raised / jnp.sum(raised, axis=1, keepdims=True)
        prob_half = probs.astype(jnp.bfloat16)
        out_block = jnp.dot(prob_half, v_win, preferred_element_type=jnp.float32).astype(
            jnp.bfloat16
        )
        delta = jnp.sum(
            g_block.astype(jnp.float32) * out_block.astype(jnp.float32), axis=1, keepdims=True
        )
        value_term = jnp.dot(prob_half.T, g_block, preferred_element_type=jnp.float32)
        prob_grad = jnp.dot(g_block, v_win.T, preferred_element_type=jnp.float32)
        score_grad = (probs * (prob_grad - delta)).astype(jnp.bfloat16)
        query_grad = (
            jnp.dot(score_grad, k_win, preferred_element_type=jnp.float32) * scale
        ).astype(jnp.bfloat16)
        key_term = jnp.dot(score_grad.T, q_block, preferred_element_type=jnp.float32) * scale
        key_acc = lax.dynamic_update_slice_in_dim(
            key_acc, lax.dynamic_slice_in_dim(key_acc, start, window, 0) + key_term, start, 0
        )
        value_acc = lax.dynamic_update_slice_in_dim(
            value_acc, lax.dynamic_slice_in_dim(value_acc, start, window, 0) + value_term, start, 0
        )
        return ((key_acc, value_acc), (out_block, query_grad))

    zeros = jnp.zeros((grand_total, head_size), jnp.float32)
    (key_acc, value_acc), (outs, grads) = lax.scan(
        step, (zeros, zeros), jnp.arange(blocks, dtype=jnp.int32)
    )
    return (outs.reshape(count, head_size), grads.reshape(count, head_size), key_acc, value_acc)


def per_device(
    upper_out,
    lower_out,
    upper_grad,
    lower_grad,
    norm_gain,
    query_weight,
    key_weight,
    value_matrix,
    out_weight,
    route_table,
    doc_lengths,
):
    lane_count = lax.axis_size("sp")
    group_count = lax.axis_size("grp")
    row_count = lower_out.shape[0]
    piece_rows = row_count // group_count
    query_width = query_weight.shape[1]
    key_value_width = key_weight.shape[1]
    q_heads = query_width // HEAD_WIDTH
    kv_heads = key_value_width // HEAD_WIDTH
    length_classes = lane_count // q_heads
    class_rows = row_count // length_classes
    class_width = class_rows * lane_count
    share_block = lane_count // kv_heads
    sequence_rows = lane_count * row_count
    full_query, full_key, full_value, full_out = (
        lax.all_gather(query_weight, "sp", axis=0, tiled=True),
        lax.all_gather(key_weight, "sp", axis=0, tiled=True),
        lax.all_gather(value_matrix, "sp", axis=0, tiled=True),
        lax.all_gather(out_weight, "sp", axis=0, tiled=True),
    )
    lower_f = lower_out.astype(jnp.float32)
    inv_rms = lax.rsqrt(jnp.mean(lower_f * lower_f, axis=1, keepdims=True) + 1e-05)
    unit = lower_f * inv_rms
    normed = (unit * norm_gain).astype(jnp.bfloat16)
    queries = jnp.dot(normed, full_query, preferred_element_type=jnp.float32).astype(jnp.bfloat16)
    key_rows = jnp.dot(normed, full_key, preferred_element_type=jnp.float32).astype(jnp.bfloat16)
    value_rows = jnp.dot(normed, full_value, preferred_element_type=jnp.float32).astype(
        jnp.bfloat16
    )
    out_grad = jnp.dot(upper_grad, full_out.T, preferred_element_type=jnp.float32).astype(
        jnp.bfloat16
    )
    packed = jnp.concatenate([queries, out_grad, key_rows, value_rows], axis=1)
    width_all = packed.shape[1]
    destiny = route_table.reshape(group_count)
    targets = jnp.arange(group_count, dtype=jnp.int32)
    match = destiny[:, None] == targets[None, :]
    chosen = jnp.sum(jnp.where(match, targets[:, None], 0), axis=0)
    outgoing = jnp.take(packed.reshape(group_count, piece_rows, width_all), chosen, axis=0)
    arrived = lax.all_to_all(outgoing, "grp", split_axis=0, concat_axis=0, tiled=True).reshape(
        row_count, width_all
    )

    def by_head(array):
        shaped = array.reshape(length_classes, class_rows, q_heads, HEAD_WIDTH).transpose(
            2, 0, 1, 3
        )
        return shaped.reshape(lane_count, class_rows, HEAD_WIDTH)

    query_side = jnp.concatenate(
        [by_head(arrived[:, :query_width]), by_head(arrived[:, query_width : 2 * query_width])],
        axis=2,
    )
    key_side = jnp.concatenate(
        [
            arrived[:, 2 * query_width : 2 * query_width + key_value_width].reshape(
                row_count, kv_heads, HEAD_WIDTH
            ),
            arrived[:, 2 * query_width + key_value_width :].reshape(
                row_count, kv_heads, HEAD_WIDTH
            ),
        ],
        axis=2,
    ).transpose(1, 0, 2)
    lane_index = lax.axis_index("sp")
    klass = lane_index % length_classes
    ends = jnp.cumsum(doc_lengths.reshape(-1))
    positions = jnp.arange(sequence_rows, dtype=jnp.int32)
    doc_ids = jnp.sum((ends[None, :] <= positions[:, None]).astype(jnp.int32), axis=1)
    head_fanout = jnp.repeat(key_side, share_block, axis=0)
    got_query, got_keys = (
        lax.all_to_all(query_side, "sp", split_axis=0, concat_axis=0, tiled=True),
        lax.all_to_all(head_fanout, "sp", split_axis=0, concat_axis=0, tiled=True),
    )
    query_rows = got_query[:, :, :HEAD_WIDTH].reshape(-1, HEAD_WIDTH)
    grad_rows = got_query[:, :, HEAD_WIDTH:].reshape(-1, HEAD_WIDTH)
    block_rows = min(512, query_rows.shape[0])
    key_values = got_keys.reshape(lane_count, length_classes, class_rows, 2 * HEAD_WIDTH).transpose(
        1, 0, 2, 3
    )
    key_values = key_values.reshape(sequence_rows, 2 * HEAD_WIDTH)
    query_pos = klass * class_width + jnp.arange(class_width, dtype=jnp.int32)
    window = min(sequence_rows, block_rows + LONGEST)
    outs, grads, key_acc, value_acc = attend(
        query_rows,
        grad_rows,
        key_values[:, :HEAD_WIDTH],
        key_values[:, HEAD_WIDTH:],
        query_pos,
        doc_ids,
        block_rows,
        window,
        LONGEST,
    )
    key_back = jnp.concatenate([key_acc, value_acc], axis=1).astype(jnp.bfloat16)
    key_back = key_back.reshape(length_classes, lane_count, class_rows, 2 * HEAD_WIDTH).transpose(
        1, 0, 2, 3
    )
    key_back = key_back.reshape(lane_count, row_count, 2 * HEAD_WIDTH)
    query_back = jnp.concatenate([outs, grads], axis=1).reshape(
        lane_count, class_rows, 2 * HEAD_WIDTH
    )
    ret_query, ret_keys = (
        lax.all_to_all(query_back, "sp", split_axis=0, concat_axis=0, tiled=True),
        lax.all_to_all(key_back, "sp", split_axis=0, concat_axis=0, tiled=True),
    )
    head_rows = ret_query.reshape(q_heads, length_classes, class_rows, 2 * HEAD_WIDTH).transpose(
        1, 2, 0, 3
    )
    head_rows = head_rows.reshape(row_count, q_heads, 2 * HEAD_WIDTH)
    attn_rows = head_rows[:, :, :HEAD_WIDTH].reshape(row_count, query_width)
    qgrad_rows = head_rows[:, :, HEAD_WIDTH:].reshape(row_count, query_width)
    key_total = jnp.sum(
        ret_keys.reshape(kv_heads, share_block, row_count, 2 * HEAD_WIDTH).astype(jnp.float32),
        axis=1,
    )
    key_total = key_total.astype(jnp.bfloat16).transpose(1, 0, 2)
    kgrad_rows = key_total[:, :, :HEAD_WIDTH].reshape(row_count, key_value_width)
    vgrad_rows = key_total[:, :, HEAD_WIDTH:].reshape(row_count, key_value_width)
    homeward = jnp.concatenate([attn_rows, qgrad_rows, kgrad_rows, vgrad_rows], axis=1)
    returned = lax.all_to_all(
        homeward.reshape(group_count, piece_rows, width_all),
        "grp",
        split_axis=0,
        concat_axis=0,
        tiled=True,
    )
    mine = jnp.take(returned, destiny, axis=0).reshape(row_count, width_all)
    attn_back = mine[:, :query_width]
    query_grad = mine[:, query_width : 2 * query_width]
    key_grad = mine[:, 2 * query_width : 2 * query_width + key_value_width]
    value_grad = mine[:, 2 * query_width + key_value_width :]
    mixed = jnp.dot(attn_back, full_out, preferred_element_type=jnp.float32)
    restored = (upper_out.astype(jnp.float32) - mixed).astype(jnp.bfloat16)
    normed_grad = jnp.dot(query_grad, full_query.T, preferred_element_type=jnp.float32)
    normed_grad = normed_grad + jnp.dot(key_grad, full_key.T, preferred_element_type=jnp.float32)
    normed_grad = normed_grad + jnp.dot(
        value_grad, full_value.T, preferred_element_type=jnp.float32
    )
    unit_grad = normed_grad * norm_gain
    lower_term = inv_rms * (unit_grad - unit * jnp.mean(unit_grad * unit, axis=1, keepdims=True))
    back_grad = (lower_grad.astype(jnp.float32) + lower_term).astype(jnp.bfloat16)
    return (restored, back_grad)


def solution(mesh):
    return jax.shard_map(
        per_device,
        mesh=mesh,
        in_specs=(
            P(("grp", "sp"), None),
            P(("grp", "sp"), None),
            P(("grp", "sp"), None),
            P(("grp", "sp"), None),
            P(),
            P("sp", None),
            P("sp", None),
            P("sp", None),
            P("sp", None),
            P("grp", "sp", None),
            P("grp", None),
        ),
        out_specs=(P(("grp", "sp"), None), P(("grp", "sp"), None)),
        check_vma=False,
    )
```

profile of v0, /device:TPU:1, one launch (start us, length us, event | category | flops | bytes accessed | tf_op | source)
XLA Modules:
  0.0 661.2 jit_solution(5510413115308153578)
XLA Ops:
  12.0 82.1 %all-gather.9.cloned.1.call-done = bf16[2048,256]{1,0:T(8,128)(2,1)} async-done(((bf16[32,256]{1,0:T(8,128)(2,1)}), bf16[2048,256]{1,0:T(8,128)(2,1)}) %all-gather.9.cloned.1.call-update) | async-done | bytes 1048592 | tf_op jit(solution)/shard_map/all_gather | solution.py:96
  95.9 80.2 %all-gather.11.cloned.1.call-done = bf16[2048,256]{1,0:T(8,128)(2,1)} async-done(((bf16[32,256]{1,0:T(8,128)(2,1)}), bf16[2048,256]{1,0:T(8,128)(2,1)}) %all-gather.11.cloned.1.call-update) | async-done | bytes 1048592 | tf_op jit(solution)/shard_map/all_gather | solution.py:97
  177.7 86.1 %all-gather.5.cloned.1.call-done = bf16[2048,1024]{1,0:T(8,128)(2,1)} async-done(((bf16[32,1024]{1,0:T(8,128)(2,1)}), bf16[2048,1024]{1,0:T(8,128)(2,1)}) %all-gather.5.cloned.1.call-update) | async-done | bytes 4194320 | tf_op jit(solution)/shard_map/all_gather | solution.py:95
  263.8 2.9 convolution_convert_fusion.2
  266.7 83.8 %all-gather.7.cloned.1.call-done = bf16[1024,2048]{1,0:T(8,128)(2,1)} async-done(((bf16[16,2048]{1,0:T(8,128)(2,1)}), bf16[1024,2048]{1,0:T(8,128)(2,1)}) %all-gather.7.cloned.1.call-update) | async-done | bytes 4194320 | tf_op jit(solution)/shard_map/all_gather | solution.py:98
  350.5 3.7 convolution_convert_fusion.1
  355.0 19.6 %all_to_all.30 = bf16[8,16,2560]{2,1,0:T(8,128)(2,1)S(1)} all-to-all(bf16[8,16,2560]{2,1,0:T(8,128)(2,1)S(1)} %broadcast_select_fusion.1), channel_id=1, replica_groups=mesh['grp'=8,'sp'=64] {'grp'}, dimensions={0} | all-to-all | bytes 1310720 | tf_op jit(solution)/shard_map/all_to_all | solution.py:119
  376.7 8.4 %all-to-all-start.1 = ((bf16[64,32,128]{2,1,0:T(8,128)(2,1)}), bf16[64,32,128]{2,1,0:T(8,128)(2,1)S(1)}, u32[]{:S(2)}, u32[]{:S(2)}) async-start(bf16[64,32,128]{2,1,0:T(8,128)(2,1)} %pad_maximum_fusion.2), calls=%async_computation.1 | async-start | bytes 1048576 | tf_op jit(solution)/shard_map/all_to_all | solution.py:151
  385.6 16.6 %all-to-all-done.1 = bf16[64,32,128]{2,1,0:T(8,128)(2,1)S(1)} async-done(((bf16[64,32,128]{2,1,0:T(8,128)(2,1)}), bf16[64,32,128]{2,1,0:T(8,128)(2,1)S(1)}, u32[]{:S(2)}, u32[]{:S(2)}) %all-to-all-start.1) | async-done | bytes 524320 | tf_op jit(solution)/shard_map/all_to_all | solution.py:151
  404.0 7.1 %all-to-all-start.2 = ((bf16[64,128,128]{2,1,0:T(8,128)(2,1)}), bf16[64,128,128]{2,1,0:T(8,128)(2,1)S(1)}, u32[]{:S(2)}, u32[]{:S(2)}) async-start(bf16[64,128,128]{2,1,0:T(8,128)(2,1)} %bitcast.72), calls=%async_computation.2 | async-start | bytes 4194304 | tf_op jit(solution)/shard_map/all_to_all | solution.py:152
  414.1 45.8 %all-to-all-done.2 = bf16[64,128,128]{2,1,0:T(8,128)(2,1)S(1)} async-done(((bf16[64,128,128]{2,1,0:T(8,128)(2,1)}), bf16[64,128,128]{2,1,0:T(8,128)(2,1)S(1)}, u32[]{:S(2)}, u32[]{:S(2)}) %all-to-all-start.2) | async-done | bytes 2097184 | tf_op jit(solution)/shard_map/all_to_all | solution.py:152
  460.3 2.7 fusion.45
  464.6 73.1 %while.20 = (s32[]{:T(128)}, f32[8192,64]{0,1:T(8,128)}, f32[8192,64]{0,1:T(8,128)S(1)}, bf16[4,512,64]{1,2,0:T(8,128)(2,1)}, bf16[4,512,64]{1,2,0:T(8,128)(2,1)...) while((s32[]{:T(128)}, f32[8192,64]{0,1:T(8,128)}, ...), condition=%wide.region_8.10_spmd, body=%wide.region_4.9_spmd.sunk | while | flops 410949120 | bytes 21758800 | solution.py:62
  467.1 3.1 gather_fusion
  476.9 2.0 fusion.87
  485.0 3.1 gather_fusion
  494.8 2.0 fusion.87
  498.2 2.0 dynamic_update_slice.45
  503.4 3.1 gather_fusion
  513.2 2.0 fusion.87
  516.6 2.0 dynamic_update_slice.45
  521.8 3.1 gather_fusion
  531.6 2.0 fusion.87
  540.8 2.1 pad_maximum_fusion.3
  543.0 10.4 %all-to-all-start.3 = ((bf16[64,32,128]{2,1,0:T(8,128)(2,1)}), bf16[64,32,128]{2,1,0:T(8,128)(2,1)S(1)}, u32[]{:S(2)}, u32[]{:S(2)}) async-start(bf16[64,32,128]{2,1,0:T(8,128)(2,1)} %pad_maximum_fusion.3), calls=%async_computation.3 | async-start | bytes 1048576 | tf_op jit(solution)/shard_map/all_to_all | solution.py:183
  553.4 2.9 copy.83
  558.2 3.4 maximum_bitcast_fusion
  563.6 6.4 all-to-all-done.3
  570.0 7.2 %all-to-all-start.4 = ((bf16[64,128,128]{2,1,0:T(8,128)(2,1)}), bf16[64,128,128]{2,1,0:T(8,128)(2,1)S(1)}, u32[]{:S(2)}, u32[]{:S(2)}) async-start(bf16[64,128,128]{2,1,0:T(8,128)(2,1)} %bitcast.29), calls=%async_computation.4 | async-start | bytes 4194304 | tf_op jit(solution)/shard_map/all_to_all | solution.py:184
  581.0 44.3 %all-to-all-done.4 = bf16[64,128,128]{2,1,0:T(8,128)(2,1)S(1)} async-done(((bf16[64,128,128]{2,1,0:T(8,128)(2,1)}), bf16[64,128,128]{2,1,0:T(8,128)(2,1)S(1)}, u32[]{:S(2)}, u32[]{:S(2)}) %all-to-all-start.4) | async-done | bytes 2097184 | tf_op jit(solution)/shard_map/all_to_all | solution.py:184
  627.3 8.7 %all-to-all-start.5 = ((bf16[8,16,2560]{2,1,0:T(8,128)(2,1)}), bf16[8,16,2560]{2,1,0:T(8,128)(2,1)S(1)}, u32[]{:S(2)}, u32[]{:S(2)}) async-start(bf16[8,16,2560]{2,1,0:T(8,128)(2,1)} %pad_maximum_fusion.1), calls=%async_computation.5 | async-start | bytes 1310720 | tf_op jit(solution)/shard_map/all_to_all | solution.py:200
  636.1 10.9 %all-to-all-done.5 = bf16[8,16,2560]{2,1,0:T(8,128)(2,1)S(1)} async-done(((bf16[8,16,2560]{2,1,0:T(8,128)(2,1)}), bf16[8,16,2560]{2,1,0:T(8,128)(2,1)S(1)}, u32[]{:S(2)}, u32[]{:S(2)}) %all-to-all-start.5) | async-done | bytes 655392 | tf_op jit(solution)/shard_map/all_to_all | solution.py:200
  (160 shorter events, 81.3 us)
Async XLA Ops:
  7.2 343.4 %copy-start = (bf16[128,2048]{1,0:T(8,128)(2,1)S(1)}, bf16[128,2048]{1,0:T(8,128)(2,1)}, u32[]{:S(2)}) copy-start(bf16[128,2048]{1,0:T(8,128)(2,1)} %param.17) | copy-start | bytes 1572868
  7.2 168.9 %copy-start.3 = (bf16[128,2048]{1,0:T(8,128)(2,1)S(1)}, bf16[128,2048]{1,0:T(8,128)(2,1)}, u32[]{:S(2)}) copy-start(bf16[128,2048]{1,0:T(8,128)(2,1)} %param.16) | copy-start | bytes 1572868
  7.2 168.9 %copy-start.9 = (f32[2048]{0:T(1024)S(1)}, f32[2048]{0:T(1024)}, u32[]{:S(2)}) copy-start(f32[2048]{0:T(1024)} %param.19) | copy-start | bytes 24580
  7.2 86.9 %all-gather.9.cloned.1.call-start = ((), (), s32[]{:S(2)}) async-start(), calls=%async_computation.8 | async-start | bytes 1064960 | tf_op jit(solution)/shard_map/all_gather | solution.py:96
  7.9 168.1 %all-gather.11.cloned.1.call-start = ((), (), s32[]{:S(2)}) async-start(), calls=%async_computation.9 | async-start | bytes 1064960 | tf_op jit(solution)/shard_map/all_gather | solution.py:97
  8.7 255.1 %all-gather.5.cloned.1.call-start = ((), (), s32[]{:S(2)}) async-start(), calls=%async_computation.6 | async-start | bytes 4259840 | tf_op jit(solution)/shard_map/all_gather | solution.py:95
  9.4 341.1 %all-gather.7.cloned.1.call-start = ((), (), s32[]{:S(2)}) async-start(), calls=%async_computation.7 | async-start | bytes 4259840 | tf_op jit(solution)/shard_map/all_gather | solution.py:98
  376.7 25.4 %all-to-all-start.1 = ((bf16[64,32,128]{2,1,0:T(8,128)(2,1)}), bf16[64,32,128]{2,1,0:T(8,128)(2,1)S(1)}, u32[]{:S(2)}, u32[]{:S(2)}) async-start(bf16[64,32,128]{2,1,0:T(8,128)(2,1)} %pad_maximum_fusion.2), calls=%async_computation.1 | async-start | bytes 1048576 | tf_op jit(solution)/shard_map/all_to_all | solution.py:151
  404.0 7.2 %copy-start.10 = (s32[1,32]{1,0:T(1,128)S(1)}, s32[1,32]{1,0:T(1,128)}, u32[]{:S(2)}) copy-start(s32[1,32]{1,0:T(1,128)} %param.25) | copy-start | bytes 388
  404.0 55.8 %all-to-all-start.2 = ((bf16[64,128,128]{2,1,0:T(8,128)(2,1)}), bf16[64,128,128]{2,1,0:T(8,128)(2,1)S(1)}, u32[]{:S(2)}, u32[]{:S(2)}) async-start(bf16[64,128,128]{2,1,0:T(8,128)(2,1)} %bitcast.72), calls=%async_computation.2 | async-start | bytes 4194304 | tf_op jit(solution)/shard_map/all_to_all | solution.py:152
  543.0 27.0 %all-to-all-start.3 = ((bf16[64,32,128]{2,1,0:T(8,128)(2,1)}), bf16[64,32,128]{2,1,0:T(8,128)(2,1)S(1)}, u32[]{:S(2)}, u32[]{:S(2)}) async-start(bf16[64,32,128]{2,1,0:T(8,128)(2,1)} %pad_maximum_fusion.3), calls=%async_computation.3 | async-start | bytes 1048576 | tf_op jit(solution)/shard_map/all_to_all | solution.py:183
  570.0 55.4 %all-to-all-start.4 = ((bf16[64,128,128]{2,1,0:T(8,128)(2,1)}), bf16[64,128,128]{2,1,0:T(8,128)(2,1)S(1)}, u32[]{:S(2)}, u32[]{:S(2)}) async-start(bf16[64,128,128]{2,1,0:T(8,128)(2,1)} %bitcast.29), calls=%async_computation.4 | async-start | bytes 4194304 | tf_op jit(solution)/shard_map/all_to_all | solution.py:184
  581.0 45.3 %copy-start.5 = (bf16[8,16,1024]{2,1,0:T(8,128)(2,1)S(1)}, bf16[8,16,1024]{2,1,0:T(8,128)(2,1)}, u32[]{:S(2)}) copy-start(bf16[8,16,1024]{2,1,0:T(8,128)(2,1)} %concatenate.45) | copy-start | bytes 786436
  625.7 10.3 %copy-start.11 = (s32[1,1,8]{2,1,0:T(1,128)S(1)}, s32[1,1,8]{2,1,0:T(1,128)}, u32[]{:S(2)}) copy-start(s32[1,1,8]{2,1,0:T(1,128)} %param.24) | copy-start | bytes 100
  627.3 19.6 %all-to-all-start.5 = ((bf16[8,16,2560]{2,1,0:T(8,128)(2,1)}), bf16[8,16,2560]{2,1,0:T(8,128)(2,1)S(1)}, u32[]{:S(2)}, u32[]{:S(2)}) async-start(bf16[8,16,2560]{2,1,0:T(8,128)(2,1)} %pad_maximum_fusion.1), calls=%async_computation.5 | async-start | bytes 1310720 | tf_op jit(solution)/shard_map/all_to_all | solution.py:200
  636.0 13.5 %copy-start.6 = (bf16[2048,256]{1,0:T(8,128)(2,1)S(1)}, bf16[2048,256]{1,0:T(8,128)(2,1)}, u32[]{:S(2)}) copy-start(bf16[2048,256]{1,0:T(8,128)(2,1)} %all-gather.9.cloned.1.call-done) | copy-start | bytes 3145732
  647.5 2.5 copy-start.4
  647.7 2.6 copy-start.1
  650.2 1.7 copy-start.7
  650.2 2.9 copy-start.2
  651.9 1.2 copy-start.8
Sparse Core Ops, SparseCore 0:
  11.1 82.9 all-gather.8
  97.2 78.8 all-gather.10
  179.2 84.5 all-gather.4
  266.7 83.8 all-gather.6
where the time goes:
time: 663 us; the launch traced here: 661 us
  waiting for transfers between devices  459 us (69%)
  local copies, waits for them, and re-layouts  56.3 us (8%)
  matrix products  48.6 us (7%)
  starting transfers between devices  42.1 us (6%)
  blocking collectives  19.6 us (3%)
  other arithmetic  16.2 us (2%)
  between operations  14.2 us (2%)
    all_gather x1, waiting for transfers between devices, per_device(): lax.all_gather(query_weight, 'sp', axis=0, tiled=True)  86.1 us
    all_gather x1, waiting for transfers between devices, per_device(): lax.all_gather(out_weight, 'sp', axis=0, tiled=True)  83.8 us
    all_gather x1, waiting for transfers between devices, per_device(): lax.all_gather(key_weight, 'sp', axis=0, tiled=True)  82.1 us
    all_gather x1, waiting for transfers between devices, per_device(): lax.all_gather(value_matrix, 'sp', axis=0, tiled=True)  80.2 us
    all_to_all x1, waiting for transfers between devices, per_device(): lax.all_to_all(head_fanout, 'sp', split_axis=0, concat_axis=0, tiled=True)  45.8 us
    all_to_all x1, waiting for transfers between devices, per_device(): lax.all_to_all(key_back, 'sp', split_axis=0, concat_axis=0, tiled=True)  44.3 us
    all_to_all x1, blocking collectives, per_device(): lax.all_to_all(outgoing, 'grp', split_axis=0, concat_axis=0, tiled=True)  19.6 us
    all_to_all x1, waiting for transfers between devices, per_device(): lax.all_to_all(query_side, 'sp', split_axis=0, concat_axis=0, tiled=True)  16.6 us
  transfers between devices with their start and end apart: 9, of which 9 were waited for; matrix products, arithmetic and copies ran while one was open for 4% of the time, Pallas kernels for 0%

commit v1 on v0

v1 whole, which is shorter than its diff:
```python
import functools

import jax
import jax.numpy as jnp
from jax import lax
from jax.experimental import pallas as pl
from jax.experimental.pallas import tpu as pltpu
from jax.sharding import PartitionSpec as P

HEAD = 64
PAIR = 2 * HEAD
PIECE = 16
BLOCK = 512
TILE = 128
WINDOW = BLOCK + TILE
RING = 8
HEADS_KV = 4
GROUP_COLS = 4 * PAIR + PAIR
QKV_COLS = 4 * HEAD + PAIR
MESH = pl.DeviceIdType.MESH
F32 = jnp.float32
BF16 = jnp.bfloat16


def dot(a, b):
    return jnp.dot(a, b, preferred_element_type=F32)


def dot_nt(a, b):
    return lax.dot_general(a, b, (((1,), (1,)), ((), ())), preferred_element_type=F32)


def dot_tn(a, b):
    return lax.dot_general(a, b, (((0,), (0,)), ((), ())), preferred_element_type=F32)


class Place:
    def __init__(self):
        self.g = lax.axis_index("grp")
        self.s = lax.axis_index("sp")
        self.x, self.core = self.g // 2, self.g % 2
        self.z, self.y = self.s // RING, self.s % RING
        self.zp, self.zb = self.z // 2, self.z % 2
        self.block = self.x * 4 + self.zp
        self.a = self.y
        self.c = self.core + 2 * self.zb
        self.mine = self.c * 8 + self.a
        self.source = self.zb * 16 + self.y * 2 + self.core

    def attender(self, block, c, a):
        return {"grp": (block // 4) * 2 + c % 2, "sp": ((block % 4) * 2 + c // 2) * RING + a}

    def home(self, block, source):
        return {
            "grp": (block // 4) * 2 + source % 2,
            "sp": ((block % 4) * 2 + source // 16) * RING + (source // 2) % RING,
        }

    def after(self):
        return (self.block + 1) % 16

    def before(self):
        return (self.block + 15) % 16


def greet(at):
    barrier = pltpu.get_barrier_semaphore()

    def signal(device):
        pl.semaphore_signal(barrier, inc=1, device_id=device, device_id_type=MESH)

    for dz in (1, RING - 1):
        signal({"grp": at.g, "sp": ((at.z + dz) % RING) * RING + at.y})
    for d in range(1, 8):
        signal({"grp": (at.g + d) % 8, "sp": at.s})

    def own(d, carry):
        other = (at.mine + d) % 32
        signal(at.attender(at.block, other // 8, other % 8))
        return carry

    def both(d, carry):
        other = (at.mine + d) % 32
        signal(at.attender(at.after(), other // 8, other % 8))
        signal(at.attender(at.before(), other // 8, other % 8))
        return carry

    lax.fori_loop(1, 32, own, 0)
    lax.fori_loop(0, 32, both, 0)
    pl.semaphore_wait(barrier, 2 + 7 + 31 + 64)


class Gather:
    def __init__(self, at, full, sems):
        self.at, self.full = at, full
        self.out_sem, self.in_sem, self.share_out, self.share_in = sems
        self.count = 0
        self.pending = []

    def first_block(self, order, core, index, part):
        rows = slice(None) if part is None else pl.ds(PIECE * part, PIECE)
        j = 2 * core + order
        if order == 0:
            return self.full.at[j, self.at.z, index, rows]
        return self.full.at[j, index, self.at.y, rows]

    def second_block(self, order, core, index, part):
        j = 2 * core + order
        if order == 0:
            return self.full.at[j, index, pl.ds(4 * part, 4)]
        return self.full.at[j, pl.ds(4 * part, 4), index]

    def ring(self, order, phase, step):
        at = self.at
        if (order + phase) % 2 == 0:
            return {"grp": at.g, "sp": at.z * RING + (at.y + step) % RING}
        return {"grp": at.g, "sp": ((at.z + step) % RING) * RING + at.y}

    def position(self, order, phase):
        return self.at.y if (order + phase) % 2 == 0 else self.at.z

    def send(self, key, block, device):
        n = self.count
        self.count += 1
        copy = pltpu.make_async_remote_copy(
            src_ref=block, dst_ref=block, send_sem=self.out_sem.at[n], recv_sem=self.in_sem.at[n],
            device_id=device, device_id_type=MESH,
        )
        copy.start()
        self.pending.append((copy, n))
        return n

    def receive(self, n, block, sibling_block):
        at = self.at
        sibling = {"grp": at.x * 2 + 1 - at.core, "sp": at.s}
        pltpu.make_async_remote_copy(
            src_ref=block, dst_ref=block, send_sem=self.out_sem.at[n], recv_sem=self.in_sem.at[n],
            device_id=sibling, device_id_type=MESH,
        ).wait_recv()
        share = pltpu.make_async_remote_copy(
            src_ref=block, dst_ref=block, send_sem=self.share_out.at[n],
            recv_sem=self.share_in.at[n], device_id=sibling, device_id_type=MESH,
        )
        share.start()
        self.shares.append((share, n, sibling_block))

    def run(self, between):
        at = self.at
        self.shares = []
        for phase in (0, 1):
            slots = {}
            blocks = self.first_block if phase == 0 else self.second_block
            parts = (None,) if phase == 0 else (0, 1)
            for step in range(1, 6):
                for half, part in enumerate(parts):
                    for order in (0, 1):
                        here = self.position(order, phase)
                        for way in (1, -1):
                            def chunk(t):
                                if t < 4:
                                    return part
                                if phase == 0:
                                    return 0 if way == 1 else 1
                                return part if (part == 0) == (way == 1) else -1

                            if step > 1:
                                piece = chunk(step - 1)
                                if piece != -1:
                                    index = (here - way * (step - 1) + RING) % RING
                                    n = slots[(half, order, way, step - 1)]
                                    self.receive(
                                        n,
                                        blocks(order, at.core, index, piece),
                                        blocks(order, 1 - at.core, index, piece),
                                    )
                            if step < 5:
                                piece = chunk(step)
                                if piece != -1:
                                    index = (here - way * (step - 1) + RING) % RING
                                    slots[(half, order, way, step)] = self.send(
                                        None,
                                        blocks(order, at.core, index, piece),
                                        self.ring(order, phase, way),
                                    )
                if phase == 0 and step == 1:
                    between()

    def shared(self):
        for share, n, block in self.shares:
            pltpu.make_async_copy(block, block, self.share_in.at[n]).wait()

    def drain(self):
        for copy, _ in self.pending:
            copy.wait_send()
        for share, _, _ in self.shares:
            share.wait_send()


def attention(at, recv, halo, keys, total, back, ends_ref):
    low = lax.broadcasted_iota(jnp.int32, (1, PAIR), 1) < HEAD
    pick_query = jnp.where(low, 0.125, 0.0).astype(BF16)
    pick_grad = jnp.where(low, 0.0, 1.0).astype(BF16)
    low_rows = lax.broadcasted_iota(jnp.int32, (PAIR, TILE), 0) < HEAD
    keys[pl.ds(0, BLOCK), :] = halo[...]
    keys[pl.ds(BLOCK, BLOCK), :] = recv[:, 4 * PAIR :]
    total[...] = jnp.zeros_like(total)
    ends = ends_ref[...]

    def tile(t, carry):
        first = pl.multiple_of(t * TILE, TILE)
        both = jnp.concatenate(
            [recv[pl.ds(first, TILE), PAIR * h : PAIR * (h + 1)] for h in range(4)], axis=0
        )
        queries = both * pick_query
        grads = both * pick_grad
        window = keys[pl.ds(first, WINDOW), :]
        window_t = window.T
        scores = dot_nt(window, queries)
        prob_grad = dot_nt(window, grads)
        position = at.block * BLOCK + first + lax.broadcasted_iota(jnp.int32, (1, TILE), 1)
        began = jnp.max(jnp.where(ends <= position, ends, 0), axis=0, keepdims=True)
        key_position = (at.block - 1) * BLOCK + first + lax.broadcasted_iota(
            jnp.int32, (WINDOW, TILE), 0
        )
        allowed = (key_position >= began) & (key_position <= position)
        halves, slopes = [], []
        for h in range(4):
            cols = slice(TILE * h, TILE * (h + 1))
            s = jnp.where(allowed, scores[:, cols], -jnp.inf)
            raised = jnp.exp(s - jnp.max(s, axis=0, keepdims=True))
            probs = raised * (1.0 / jnp.sum(raised, axis=0, keepdims=True))
            half = probs.astype(BF16)
            out_t = dot(window_t, half).astype(BF16).astype(F32)
            grad_t = grads[cols, :].astype(F32).T
            delta = jnp.sum(grad_t * out_t, axis=0, keepdims=True)
            slope = (probs * (prob_grad[:, cols] - delta)).astype(BF16)
            query_grad = dot(window_t, slope) * 0.125
            result = jnp.where(low_rows, query_grad, out_t).T.astype(BF16)
            back[pl.ds(first, TILE), PAIR * h : PAIR * (h + 1)] = result
            halves.append(half)
            slopes.append(slope)
        total[pl.ds(first, WINDOW), :] += dot(
            jnp.concatenate(slopes, axis=1), queries
        ) + dot(jnp.concatenate(halves, axis=1), grads)
        return carry

    lax.fori_loop(0, BLOCK // TILE, tile, 0)
    back[:, 4 * PAIR :] = total[pl.ds(BLOCK, BLOCK), :].astype(BF16)


def swap_halves(a):
    return pltpu.roll(a, HEAD, 1)


def kernel(
    lower_ref, ugrad_ref, uout_ref, lgrad_ref, gain_ref, shard_ref, dest_ref, ends_in,
    restored_ref, backg_ref,
    full, normed, send, recv, halo, keys, total, back, back_halo, ret, ret_halo, ends,
    g_out, g_in, h_out, h_in, sems,
):
    at = Place()
    rows = lower_ref.shape[0]
    greet(at)

    @pl.when(at.y == at.g)
    def _():
        def tell(d, carry):
            pltpu.make_async_remote_copy(
                src_ref=ends_in, dst_ref=ends, send_sem=sems.at[0], recv_sem=sems.at[1],
                device_id={"grp": (at.g + d) % 8, "sp": at.s}, device_id_type=MESH,
            ).start()
            return carry

        lax.fori_loop(1, 8, tell, 0)
        ends[...] = ends_in[...]

    for j in range(HEADS_KV):
        full[j, at.z, at.y] = shard_ref[j]

    def inverse_rms():
        low = lower_ref[...].astype(F32)
        return low, lax.rsqrt(jnp.mean(low * low, axis=1, keepdims=True) + 1e-05)

    def norm():
        low, inv = inverse_rms()
        normed[...] = ((low * inv) * gain_ref[...]).astype(BF16)

    gather = Gather(at, full, (g_out, g_in, h_out, h_in))
    gather.run(norm)
    gather.shared()

    def out_half(j, h):
        return full[j, :, :, PIECE * h : PIECE * (h + 1), QKV_COLS:].reshape(
            QUERY_COLS, GROUP_COLS - QKV_COLS
        )

    QUERY_COLS = HEADS_KV * 4 * HEAD
    deep = RING * RING * 32
    permute = (
        lax.broadcasted_iota(jnp.int32, (rows, rows), 0) == dest_ref[...]
    ).astype(F32).astype(BF16)
    low = lax.broadcasted_iota(jnp.int32, (rows, PAIR), 1) < HEAD

    grad_cols = jnp.zeros((rows, QUERY_COLS), F32)
    for j in range(HEADS_KV):
        for h in range(2):
            first = 512 * j + 256 * h
            grad_cols = grad_cols + dot_nt(ugrad_ref[:, first : first + 256], out_half(j, h))
    for c in range(HEADS_KV):
        qkv = dot(normed[...], full[c, :, :, :, :QKV_COLS].reshape(deep, QKV_COLS))
        parts = []
        for p in range(2):
            q2 = qkv[:, PAIR * p : PAIR * (p + 1)]
            g2 = grad_cols[:, 256 * c + PAIR * p : 256 * c + PAIR * (p + 1)]
            parts.append(jnp.where(low, q2, swap_halves(g2)).astype(BF16))
            parts.append(jnp.where(low, swap_halves(q2), g2).astype(BF16))
        parts.append(qkv[:, 4 * HEAD :].astype(BF16))
        send[c] = dot(permute, jnp.concatenate(parts, axis=1)).astype(BF16)

    def piece(i):
        return pl.ds(pl.multiple_of(i * PIECE, PIECE), PIECE)

    kv_cols = pl.ds(4 * PAIR, PAIR)
    local = pltpu.make_async_copy(
        send.at[at.c, piece(at.a), :], recv.at[piece(at.source), :], sems.at[3]
    )
    local.start()

    def send_own(d, carry):
        other = (at.mine + d) % 32
        c, a = other // 8, other % 8
        pltpu.make_async_remote_copy(
            src_ref=send.at[c, piece(a), :], dst_ref=recv.at[piece(at.source), :],
            send_sem=sems.at[2], recv_sem=sems.at[3],
            device_id=at.attender(at.block, c, a), device_id_type=MESH,
        ).start()
        return carry

    def send_halo(d, carry):
        other = (at.mine + d) % 32
        c, a = other // 8, other % 8
        pltpu.make_async_remote_copy(
            src_ref=send.at[c, piece(a), kv_cols], dst_ref=halo.at[piece(at.source), :],
            send_sem=sems.at[4], recv_sem=sems.at[5],
            device_id=at.attender(at.after(), c, a), device_id_type=MESH,
        ).start()
        return carry

    lax.fori_loop(0, 32, send_halo, 0)
    lax.fori_loop(1, 32, send_own, 0)

    def wait_bytes(ref, sem):
        pltpu.make_async_copy(ref, ref, sem).wait()

    @pl.when(at.y != at.g)
    def _():
        wait_bytes(ends, sems.at[1])

    wait_bytes(halo, sems.at[5])
    wait_bytes(recv, sems.at[3])
    attention(at, recv, halo, keys, total, back, ends)
    back_halo[...] = total[pl.ds(0, BLOCK), :].astype(BF16)

    local_back = pltpu.make_async_copy(
        back.at[piece(at.source), :], ret.at[at.c, piece(at.a), :], sems.at[7]
    )
    local_back.start()

    def return_own(d, carry):
        source = (at.source + d) % 32
        pltpu.make_async_remote_copy(
            src_ref=back.at[piece(source), :], dst_ref=ret.at[at.c, piece(at.a), :],
            send_sem=sems.at[6], recv_sem=sems.at[7],
            device_id=at.home(at.block, source), device_id_type=MESH,
        ).start()
        return carry

    def return_halo(d, carry):
        source = (at.source + d) % 32
        pltpu.make_async_remote_copy(
            src_ref=back_halo.at[piece(source), :], dst_ref=ret_halo.at[at.c, piece(at.a), :],
            send_sem=sems.at[8], recv_sem=sems.at[9],
            device_id=at.home(at.before(), source), device_id_type=MESH,
        ).start()
        return carry

    lax.fori_loop(0, 32, return_halo, 0)
    lax.fori_loop(1, 32, return_own, 0)
    wait_bytes(ret_halo, sems.at[9])
    wait_bytes(ret, sems.at[7])

    normed_grad = jnp.zeros((rows, deep), F32)
    attended = []
    for c in range(HEADS_KV):
        got = ret[c]
        kv = (got[:, 4 * PAIR :].astype(F32) + ret_halo[c].astype(F32)).astype(BF16)
        mine = dot_tn(permute, jnp.concatenate([got[:, : 4 * PAIR], kv], axis=1))
        slopes = []
        for p in range(2):
            even = mine[:, 2 * PAIR * p : 2 * PAIR * p + PAIR]
            odd = mine[:, 2 * PAIR * p + PAIR : 2 * PAIR * (p + 1)]
            slopes.append(jnp.where(low, even, swap_halves(odd)).astype(BF16))
            attended.append(jnp.where(low, swap_halves(even), odd).astype(BF16))
        slopes.append(mine[:, 4 * PAIR :].astype(BF16))
        normed_grad = normed_grad + dot_nt(
            jnp.concatenate(slopes, axis=1),
            full[c, :, :, :, :QKV_COLS].reshape(deep, QKV_COLS),
        )
    attended = jnp.concatenate(attended, axis=1)
    for j in range(HEADS_KV):
        for h in range(2):
            first = 512 * j + 256 * h
            mixed = dot(attended, out_half(j, h))
            restored_ref[:, first : first + 256] = (
                uout_ref[:, first : first + 256].astype(F32) - mixed
            ).astype(BF16)
    low_f, inv = inverse_rms()
    unit = low_f * inv
    unit_grad = normed_grad * gain_ref[...]
    term = inv * (unit_grad - unit * jnp.mean(unit_grad * unit, axis=1, keepdims=True))
    backg_ref[...] = (lgrad_ref[...].astype(F32) + term).astype(BF16)

    gather.drain()
    wait_bytes(recv.at[pl.ds(0, 31 * PIECE), :], sems.at[2])
    wait_bytes(halo, sems.at[4])
    wait_bytes(recv.at[pl.ds(0, 31 * PIECE), :], sems.at[6])
    wait_bytes(halo, sems.at[8])

    @pl.when(at.y == at.g)
    def _():
        wait_bytes(halo.at[pl.ds(0, 448), :], sems.at[0])


def per_device(
    upper_out, lower_out, upper_grad, lower_grad, norm_gain, query_weight, key_weight,
    value_matrix, out_weight, route_table, doc_lengths,
):
    rows, width = lower_out.shape
    shard = []
    for j in range(HEADS_KV):
        q = query_weight[:, 256 * j : 256 * (j + 1)]
        k = key_weight[:, HEAD * j : HEAD * (j + 1)]
        v = value_matrix[:, HEAD * j : HEAD * (j + 1)]
        o = out_weight[:, 512 * j : 512 * (j + 1)]
        o = jnp.concatenate([o[:, :256], o[:, 256:]], axis=0)
        shard.append(jnp.concatenate([q, k, v, o], axis=1))
    shard = jnp.stack(shard)
    routed = jnp.repeat(route_table.reshape(-1), PIECE) * PIECE
    dest = (routed + jnp.arange(rows, dtype=jnp.int32) % PIECE).reshape(1, rows)
    lens = doc_lengths.reshape(-1)
    docs = lens.shape[0]
    order = jnp.arange(docs, dtype=jnp.int32)
    ends = jnp.sum(jnp.where(order[None, :] <= order[:, None], lens[None, :], 0), axis=1)
    ends = jnp.broadcast_to(ends[:, None], (docs, TILE))

    vmem = pl.BlockSpec(memory_space=pltpu.VMEM)
    dma = pltpu.SemaphoreType.DMA
    return pl.pallas_call(
        kernel,
        out_shape=(jax.ShapeDtypeStruct((rows, width), BF16),) * 2,
        in_specs=[vmem] * 8,
        out_specs=(vmem, vmem),
        scratch_shapes=[
            pltpu.VMEM((HEADS_KV, RING, RING, 32, GROUP_COLS), BF16),
            pltpu.VMEM((rows, width), BF16),
            pltpu.VMEM((HEADS_KV, rows, GROUP_COLS), BF16),
            pltpu.VMEM((BLOCK, GROUP_COLS), BF16),
            pltpu.VMEM((BLOCK, PAIR), BF16),
            pltpu.VMEM((2 * BLOCK, PAIR), BF16),
            pltpu.VMEM((2 * BLOCK, PAIR), F32),
            pltpu.VMEM((BLOCK, GROUP_COLS), BF16),
            pltpu.VMEM((BLOCK, PAIR), BF16),
            pltpu.VMEM((HEADS_KV, rows, GROUP_COLS), BF16),
            pltpu.VMEM((HEADS_KV, rows, PAIR), BF16),
            pltpu.VMEM((docs, TILE), jnp.int32),
            dma((48,)), dma((48,)), dma((48,)), dma((48,)), dma((10,)),
        ],
        compiler_params=pltpu.CompilerParams(
            collective_id=0, has_side_effects=True, vmem_limit_bytes=56 * 1024 * 1024
        ),
        name="coupling",
    )(
        lower_out, upper_grad, upper_out, lower_grad, norm_gain.reshape(1, width), shard, dest, ends
    )


def solution(mesh):
    rows = P(("grp", "sp"), None)
    return jax.shard_map(
        per_device,
        mesh=mesh,
        in_specs=(
            rows, rows, rows, rows, P(), P("sp", None), P("sp", None), P("sp", None),
            P("sp", None), P("grp", "sp", None), P("grp", None),
        ),
        out_specs=(rows, rows),
        check_vma=False,
    )
```

time: 663 us -> 130 us (0.20)
  waiting for transfers between devices: 459 us -> 0 us
  Pallas kernels: 0 us -> 121 us
  local copies, waits for them, and re-layouts: 56.3 us -> 5.9 us
  matrix products: 48.6 us -> 0 us
  starting transfers between devices: 42.1 us -> 0 us
  blocking collectives: 19.6 us -> 0 us
  other arithmetic: 16.2 us -> 1.5 us
  between operations: 14.2 us -> 0.68 us
    all_gather x4 -> x0, waiting for transfers between devices: 332 us -> none  [the longest x1 86.1 us: per_device(): lax.all_gather(query_weight, 'sp', axis=0, tiled=True)]
    all_to_all x5 -> x0, waiting for transfers between devices: 124 us -> none  [the longest x1 45.8 us: per_device(): lax.all_to_all(head_fanout, 'sp', split_axis=0, concat_axis=0, tiled=True)]
    pallas_call x0 -> x1, Pallas kernels: none -> 121 us  [per_device(): pl.pallas_call(kernel, out_shape=(jax.ShapeDtypeStruct((rows, width), BF1...]
    dot_general x32 -> x0, matrix products: 48.6 us -> none  [the longest x4 8.14 us: step(): jnp.dot(score_grad, k_win, preferred_element_type=jnp.float32) * scale]
    all_to_all x5 -> x0, starting transfers between devices: 41.9 us -> none  [the longest x1 10.4 us: per_device(): lax.all_to_all(query_back, 'sp', split_axis=0, concat_axis=0, tiled=True)]
    all_to_all x1 -> x0, blocking collectives: 19.6 us -> none  [per_device(): lax.all_to_all(outgoing, 'grp', split_axis=0, concat_axis=0, tiled=True)]
    gather x6 -> x0, local copies, waits for them, and re-layouts: 13.7 us -> none  [the longest x4 12.6 us: step(): q_doc = jnp.take(doc_ids, p_block)]
    dynamic_update_slice x12 -> x0, local copies, waits for them, and re-layouts: 12.7 us -> none  [the longest x4 7.93 us: step(): lax.dynamic_update_slice_in_dim(key_acc, lax.dynamic_slice_in_dim(key_acc...]
  transfers between devices with their start and end apart: 9 -> 0, of which waited for: 9 -> 0; matrix products, arithmetic and copies ran while one was open for 4% -> 0% of each run, Pallas kernels for 0% -> 0%
where the time goes in v1:
time: 130 us
  Pallas kernels  121 us (93%)
  local copies, waits for them, and re-layouts  5.9 us (5%)
  other arithmetic  1.5 us (1%)
    pallas_call x1, Pallas kernels, per_device(): pl.pallas_call(kernel, out_shape=(jax.ShapeDtypeStruct((rows, width), BF1...  121 us
    unnamed x16, local copies, waits for them, and re-layouts  4.91 us

profile of v1, /device:TPU:1, one launch (start us, length us, event | category | flops | bytes accessed | tf_op | source)
XLA Modules:
  0.0 129.6 jit_solution(5949941610041726247)
XLA Ops:
  0.6 0.0 copy-start.5
  0.6 0.0 copy-start.6
  0.7 0.6 copy-done.5
  1.3 0.0 copy-start.3
  1.3 0.0 copy-done.6
  1.3 0.1 select_reduce_fusion
  1.4 0.1 broadcast_in_dim.25
  1.5 0.1 mul.25
  1.6 0.5 fusion.dest_ref
  2.1 0.0 copy-start.4
  2.1 0.7 broadcast_in_dim.29.ends_in
  2.8 0.0 copy-done.3
  2.8 0.0 copy-start.1
  2.8 0.1 fusion.3
  2.8 0.0 copy-done.4
  2.8 0.1 fusion.4
  2.9 0.7 copy-done.1
  3.6 0.0 copy-start.2
  3.6 0.8 copy-done.2
  4.5 0.1 maximum_bitcast_fusion
  4.5 0.1 maximum_bitcast_fusion.2
  4.6 0.7 pad_maximum_fusion.shard_ref
  5.3 121.5 %coupling.1 = (bf16[128,2048]{1,0:T(8,128)(2,1)}, bf16[128,2048]{1,0:T(8,128)(2,1)}) custom-call(bf16[128,2048]{1,0:T(8,128)(2,1)} %lower_ref.1, bf16[128,2048]{1,0:T(8,128)(2,1)} %ugrad_ref.1, bf16[128,2048]{1,0:T(8,128)(2,1)} %uout_ref.1, bf16[128,2048]{1,0:T(8,128)(2,1)} %lgrad_ref.1, f32[1,2048]{1,0:T(1,128)} %bitcast.12, ...), custom_call_target="tpu_custom_call" | custom-call | tf_op jit(solution)/shard_map/coupling/pallas_call | solution.py:458
  126.8 0.0 copy-start
  126.8 1.9 %copy.15 = bf16[128,2048]{1,0:T(8,128)(2,1)} copy(bf16[128,2048]{1,0:T(8,128)(2,1)} %get-tuple-element.28) | data formatting | bytes 1048576
  128.8 0.0 copy-done
  128.8 0.8 copy.16
  (3 shorter events, 0.0 us)
Async XLA Ops:
  0.6 0.7 copy-start.5
  0.6 0.7 copy-start.6
  1.3 1.5 %copy-start.3 = (bf16[32,256]{1,0:T(8,128)(2,1)S(1)}, bf16[32,256]{1,0:T(8,128)(2,1)}, u32[]{:S(2)}) copy-start(bf16[32,256]{1,0:T(8,128)(2,1)} %param.17) | copy-start | bytes 49156
  2.1 0.8 copy-start.4
  2.8 0.8 copy-start.1
  3.6 0.8 copy-start.2
  126.8 2.0 %copy-start = (bf16[128,2048]{1,0:T(8,128)(2,1)S(1)}, bf16[128,2048]{1,0:T(8,128)(2,1)}, u32[]{:S(2)}) copy-start(bf16[128,2048]{1,0:T(8,128)(2,1)} %get-tuple-element.29) | copy-start | bytes 1572868

commit v2 on v1

v2 whole, which is shorter than its diff:
```python
import functools

import jax
import jax.numpy as jnp
from jax import lax
from jax.experimental import pallas as pl
from jax.experimental.pallas import tpu as pltpu
from jax.sharding import PartitionSpec as P

HEAD = 64
PAIR = 2 * HEAD
PIECE = 16
BLOCK = 512
TILE = 128
WINDOW = BLOCK + TILE
RING = 8
HEADS_KV = 4
GROUP_COLS = 4 * PAIR + PAIR
QKV_COLS = 4 * HEAD + PAIR
MESH = pl.DeviceIdType.MESH
F32 = jnp.float32
BF16 = jnp.bfloat16


def dot(a, b):
    return jnp.dot(a, b, preferred_element_type=F32)


def dot_nt(a, b):
    return lax.dot_general(a, b, (((1,), (1,)), ((), ())), preferred_element_type=F32)


def dot_tn(a, b):
    return lax.dot_general(a, b, (((0,), (0,)), ((), ())), preferred_element_type=F32)


class Place:
    def __init__(self):
        self.g = lax.axis_index("grp")
        self.s = lax.axis_index("sp")
        self.x, self.core = self.g // 2, self.g % 2
        self.z, self.y = self.s // RING, self.s % RING
        self.zp, self.zb = self.z // 2, self.z % 2
        self.block = self.x * 4 + self.zp
        self.a = self.y
        self.c = self.core + 2 * self.zb
        self.mine = self.c * 8 + self.a
        self.source = self.zb * 16 + self.y * 2 + self.core

    def attender(self, block, c, a):
        return {"grp": (block // 4) * 2 + c % 2, "sp": ((block % 4) * 2 + c // 2) * RING + a}

    def home(self, block, source):
        return {
            "grp": (block // 4) * 2 + source % 2,
            "sp": ((block % 4) * 2 + source // 16) * RING + (source // 2) % RING,
        }

    def after(self):
        return (self.block + 1) % 16

    def before(self):
        return (self.block + 15) % 16


def greet(at):
    barrier = pltpu.get_barrier_semaphore()

    def signal(device):
        pl.semaphore_signal(barrier, inc=1, device_id=device, device_id_type=MESH)

    for dz in (1, RING - 1):
        signal({"grp": at.g, "sp": ((at.z + dz) % RING) * RING + at.y})
    signal(at.attender(at.after(), at.c, at.a))
    signal(at.attender(at.before(), at.c, at.a))

    def column(d, carry):
        signal({"grp": (at.g + d) % 8, "sp": at.s})
        return carry

    def own(d, carry):
        other = (at.mine + d) % 32
        signal(at.attender(at.block, other // 8, other % 8))
        return carry

    lax.fori_loop(1, 8, column, 0)
    lax.fori_loop(1, 32, own, 0)
    pl.semaphore_wait(barrier, 2 + 2 + 7 + 31)


def wait_bytes(ref, sem):
    pltpu.make_async_copy(ref, ref, sem).wait()


class Gather:
    def __init__(self, at, full, sems):
        self.at, self.full = at, full
        self.first_in, self.second_in, self.share_in, self.out = sems
        self.spot = ((at.y, at.z), (at.z, at.y))

    def shard(self, order, core, i1, i2, half):
        z, y = (i2, i1) if order == 0 else (i1, i2)
        rows = slice(None) if half is None else pl.ds(PIECE * half, PIECE)
        return self.full.at[2 * core + order, z, y, rows]

    def line(self, order, core, i2):
        j = 2 * core + order
        return self.full.at[j, i2] if order == 0 else self.full.at[j, :, i2]

    def step(self, order, axis, way):
        at = self.at
        if (order + axis) % 2 == 0:
            return {"grp": at.g, "sp": at.z * RING + (at.y + way + RING) % RING}
        return {"grp": at.g, "sp": ((at.z + way + RING) % RING) * RING + at.y}

    def first(self, order, way, t, i1):
        half = None if t < 4 else (1 - way) // 2
        block = self.shard(order, self.at.core, i1, self.spot[order][1], half)
        return pltpu.make_async_remote_copy(
            src_ref=block, dst_ref=block, send_sem=self.out.at[order],
            recv_sem=self.first_in.at[order, (1 - way) // 2, t - 1],
            device_id=self.step(order, 0, way), device_id_type=MESH,
        )

    def second(self, order, way, k, m, i2):
        half = None if m < 4 else (1 - way) // 2
        i1 = (self.spot[order][0] + k + RING) % RING
        block = self.shard(order, self.at.core, i1, i2, half)
        return pltpu.make_async_remote_copy(
            src_ref=block, dst_ref=block, send_sem=self.out.at[2 + order],
            recv_sem=self.second_in.at[order, (1 - way) // 2, (k + RING) % RING, m - 1],
            device_id=self.step(order, 1, way), device_id_type=MESH,
        )

    def share(self, order, n, block):
        at = self.at
        return pltpu.make_async_remote_copy(
            src_ref=block, dst_ref=block, send_sem=self.out.at[4 + (n >= 7) * 2 + order],
            recv_sem=self.share_in.at[order, n],
            device_id={"grp": at.x * 2 + 1 - at.core, "sp": at.s}, device_id_type=MESH,
        )

    def share_block(self, order, core, n):
        p1, p2 = self.spot[order]
        if n < 7:
            return self.shard(order, core, (p1 + n + 1) % RING, p2, None)
        return self.line(order, core, (p2 + n - 6) % RING)

    def hand_over(self, order, n):
        self.share(order, n, self.share_block(order, self.at.core, n)).start()

    def run(self, filler):
        for tick in range(9):
            for order in (0, 1):
                p1 = self.spot[order][0]
                for way in (1, -1):
                    if 1 <= tick <= 4:
                        i1 = (p1 - way * tick + RING) % RING
                        self.first(order, way, tick, i1).wait_recv()
                        if tick < 4:
                            self.hand_over(order, (-way * tick) % RING - 1)
                    if tick < 4:
                        i1 = (p1 - way * tick + RING) % RING
                        self.first(order, way, tick + 1, i1).start()
                if tick == 4:
                    self.hand_over(order, 3)
            for k in (4, 3, -3, 2, -2, 1, -1, 0):
                m = tick - abs(k) + 1
                if m < 1 or m > 5:
                    continue
                for order in (0, 1):
                    p2 = self.spot[order][1]
                    for way in (1, -1):
                        i2 = (p2 - way * (m - 1) + RING) % RING
                        if m > 1:
                            self.second(order, way, k, m - 1, i2).wait_recv()
                        if m < 5:
                            self.second(order, way, k, m, i2).start()
                        if k == 4 and 1 < m < 5:
                            self.hand_over(order, 7 + (-way * (m - 1)) % RING - 1)
                    if k == 4 and m == 5:
                        self.hand_over(order, 10)
                next(filler, None)
        for _ in filler:
            pass
        for order in (0, 1):
            for n in range(14):
                wait_bytes(
                    self.share_block(order, 1 - self.at.core, n), self.share_in.at[order, n]
                )

    def drain(self):
        for order in (0, 1):
            wait_bytes(self.full.at[0, 0, pl.ds(0, 7)], self.out.at[order])
            wait_bytes(self.full.at[0, pl.ds(0, 7)], self.out.at[2 + order])
            wait_bytes(self.full.at[0, 0, pl.ds(0, 7)], self.out.at[4 + order])
            wait_bytes(self.full.at[0, pl.ds(0, 7)], self.out.at[6 + order])


def attention(at, pair, recv, keys, total, back, ends_ref, finish):
    low = lax.broadcasted_iota(jnp.int32, (1, PAIR), 1) < HEAD
    pick_query = jnp.where(low, 0.125, 0.0).astype(BF16)
    pick_grad = jnp.where(low, 0.0, 1.0).astype(BF16)
    low_rows = lax.broadcasted_iota(jnp.int32, (PAIR, TILE), 0) < HEAD
    ends = ends_ref[...]
    heads = (2 * pair, 2 * pair + 1)

    def tile(t, carry):
        first = pl.multiple_of(t * TILE, TILE)
        both = jnp.concatenate(
            [recv[pl.ds(first, TILE), PAIR * h : PAIR * (h + 1)] for h in heads], axis=0
        )
        queries = both * pick_query
        grads = both * pick_grad
        window = keys[pl.ds(first, WINDOW), :]
        window_t = window.T
        scores = dot_nt(window, queries)
        prob_grad = dot_nt(window, grads)
        position = at.block * BLOCK + first + lax.broadcasted_iota(jnp.int32, (1, TILE), 1)
        began = jnp.max(jnp.where(ends <= position, ends, 0), axis=0, keepdims=True)
        key_position = (at.block - 1) * BLOCK + first + lax.broadcasted_iota(
            jnp.int32, (WINDOW, TILE), 0
        )
        allowed = (key_position >= began) & (key_position <= position)
        halves, slopes = [], []
        for i, h in enumerate(heads):
            cols = slice(TILE * i, TILE * (i + 1))
            s = jnp.where(allowed, scores[:, cols], -jnp.inf)
            raised = jnp.exp(s - jnp.max(s, axis=0, keepdims=True))
            probs = raised * (1.0 / jnp.sum(raised, axis=0, keepdims=True))
            half = probs.astype(BF16)
            out_t = dot(window_t, half).astype(BF16).astype(F32)
            grad_t = grads[cols, :].astype(F32).T
            delta = jnp.sum(grad_t * out_t, axis=0, keepdims=True)
            slope = (probs * (prob_grad[:, cols] - delta)).astype(BF16)
            query_grad = dot(window_t, slope) * 0.125
            result = jnp.where(low_rows, query_grad, out_t).T.astype(BF16)
            back[pl.ds(first, TILE), PAIR * h : PAIR * (h + 1)] = result
            halves.append(half)
            slopes.append(slope)
        total[pl.ds(first, WINDOW), :] += dot(
            jnp.concatenate(slopes, axis=1), queries
        ) + dot(jnp.concatenate(halves, axis=1), grads)
        finish(first)
        return carry

    lax.fori_loop(0, BLOCK // TILE, tile, 0)


def swap_halves(a):
    return pltpu.roll(a, HEAD, 1)


def kernel(
    lower_hbm, ugrad_hbm, uout_hbm, lgrad_hbm, gain_ref, wq_ref, wk_ref, wv_ref, wo_ref,
    route_ref, lens_ref,
    restored_hbm, backg_hbm,
    lower_ref, ugrad_ref, uout_ref, lgrad_ref, restored_ref, backg_ref,
    full, normed, send, recv, keys, total, back, back_halo, halo_grad, ret, ends_own, ends,
    first_in, second_in, share_in, gather_out, sems, local_sems,
):
    at = Place()
    rows, width = lower_ref.shape
    deep = RING * RING * 32
    query_cols = HEADS_KV * 4 * HEAD
    low = lax.broadcasted_iota(jnp.int32, (rows, PAIR), 1) < HEAD
    loads = [
        pltpu.make_async_copy(src, dst, local_sems.at[n])
        for n, (src, dst) in enumerate(
            ((lower_hbm, lower_ref), (ugrad_hbm, ugrad_ref), (uout_hbm, uout_ref),
             (lgrad_hbm, lgrad_ref))
        )
    ]
    for load in loads:
        load.start()

    low_w = lax.broadcasted_iota(jnp.int32, (32, PAIR), 1) < HEAD
    for j in range(HEADS_KV):
        full[j, at.z, at.y, :, : 4 * HEAD] = wq_ref[:, 256 * j : 256 * (j + 1)]
        k2 = wk_ref[:, PAIR * (j // 2) : PAIR * (j // 2 + 1)].astype(F32)
        v2 = wv_ref[:, PAIR * (j // 2) : PAIR * (j // 2 + 1)].astype(F32)
        if j % 2 == 0:
            kv = jnp.where(low_w, k2, swap_halves(v2))
        else:
            kv = jnp.where(low_w, swap_halves(k2), v2)
        full[j, at.z, at.y, :, 4 * HEAD : QKV_COLS] = kv.astype(BF16)
        for h in range(2):
            first = 512 * j + 256 * h
            full[j, at.z, at.y, PIECE * h : PIECE * (h + 1), QKV_COLS:] = wo_ref[
                :, first : first + 256
            ]
    docs = ends.shape[0]
    doc = lax.broadcasted_iota(jnp.int32, (docs, TILE), 0)
    until = jnp.zeros((docs, TILE), jnp.int32)
    so_far = 0
    for k in range(docs):
        so_far = so_far + lens_ref[0, k]
        until = jnp.where(doc == k, so_far, until)
    ends_own[...] = until
    greet(at)

    @pl.when(at.y == at.g)
    def _():
        def tell(d, carry):
            pltpu.make_async_remote_copy(
                src_ref=ends_own, dst_ref=ends, send_sem=sems.at[0], recv_sem=sems.at[1],
                device_id={"grp": (at.g + d) % 8, "sp": at.s}, device_id_type=MESH,
            ).start()
            return carry

        lax.fori_loop(1, 8, tell, 0)
        ends[...] = ends_own[...]

    def norm():
        loads[0].wait()
        for r in range(0, rows, PIECE):
            part = lower_ref[r : r + PIECE, :].astype(F32)
            inv = lax.rsqrt(jnp.mean(part * part, axis=1, keepdims=True) + 1e-05)
            normed[r : r + PIECE, :] = ((part * inv) * gain_ref[...]).astype(BF16)
            yield

    gather = Gather(at, full, (first_in, second_in, share_in, gather_out))
    gather.run(norm())
    loads[1].wait()

    def out_half(j, h):
        return full[j, :, :, PIECE * h : PIECE * (h + 1), QKV_COLS:].reshape(
            query_cols, GROUP_COLS - QKV_COLS
        )

    def piece(i):
        return pl.ds(pl.multiple_of(i * PIECE, PIECE), PIECE)

    columns = (pl.ds(0, 2 * PAIR), pl.ds(2 * PAIR, 2 * PAIR), pl.ds(4 * PAIR, PAIR))

    def put_out(part):
        cols = columns[part]

        def target(source):
            if part == 2:
                return keys.at[pl.ds(pl.multiple_of(BLOCK + source * PIECE, PIECE), PIECE), :]
            return recv.at[piece(source), cols]

        pltpu.make_async_copy(
            send.at[at.c, piece(at.a), cols], target(at.source), sems.at[4 + part]
        ).start()

        def one(d, carry):
            other = (at.mine + d) % 32
            c, a = other // 8, other % 8
            pltpu.make_async_remote_copy(
                src_ref=send.at[c, piece(a), cols], dst_ref=target(at.source),
                send_sem=sems.at[10 + part], recv_sem=sems.at[4 + part],
                device_id=at.attender(at.block, c, a), device_id_type=MESH,
            ).start()
            return carry

        lax.fori_loop(1, 32, one, 0)

    def put_back(part):
        cols = columns[part]
        pltpu.make_async_copy(
            back.at[piece(at.source), cols], ret.at[at.c, piece(at.a), cols], sems.at[7 + part]
        ).start()

        def one(d, carry):
            source = (at.source + d) % 32
            pltpu.make_async_remote_copy(
                src_ref=back.at[piece(source), cols], dst_ref=ret.at[at.c, piece(at.a), cols],
                send_sem=sems.at[13 + part], recv_sem=sems.at[7 + part],
                device_id=at.home(at.block, source), device_id_type=MESH,
            ).start()
            return carry

        lax.fori_loop(1, 32, one, 0)

    row = lax.broadcasted_iota(jnp.int32, (1, rows), 1)
    dest = row % PIECE
    for p in range(rows // PIECE):
        dest = jnp.where(row // PIECE == p, dest + route_ref[0, 0, p] * PIECE, dest)
    permute = (
        lax.broadcasted_iota(jnp.int32, (rows, rows), 0) == dest
    ).astype(F32).astype(BF16)

    query_parts = []
    for c in range(HEADS_KV):
        qkv = dot(normed[...], full[c, :, :, :, :QKV_COLS].reshape(deep, QKV_COLS))
        query_parts.append(qkv[:, : 4 * HEAD])
        send[c, :, 4 * PAIR :] = dot(permute, qkv[:, 4 * HEAD :].astype(BF16)).astype(BF16)
    put_out(2)
    grad_cols = jnp.zeros((rows, query_cols), F32)
    for j in range(HEADS_KV):
        for h in range(2):
            first = 512 * j + 256 * h
            grad_cols = grad_cols + dot_nt(ugrad_ref[:, first : first + 256], out_half(j, h))
    for p in range(2):
        for c in range(HEADS_KV):
            q2 = query_parts[c][:, PAIR * p : PAIR * (p + 1)]
            g2 = grad_cols[:, 256 * c + PAIR * p : 256 * c + PAIR * (p + 1)]
            message = jnp.concatenate(
                [
                    jnp.where(low, q2, swap_halves(g2)).astype(BF16),
                    jnp.where(low, swap_halves(q2), g2).astype(BF16),
                ],
                axis=1,
            )
            send[c, :, 2 * PAIR * p : 2 * PAIR * (p + 1)] = dot(permute, message).astype(BF16)
        put_out(p)

    own_keys, old_keys = keys.at[pl.ds(BLOCK, BLOCK), :], keys.at[pl.ds(0, BLOCK), :]
    wait_bytes(own_keys, sems.at[6])
    hand_on = pltpu.make_async_remote_copy(
        src_ref=own_keys, dst_ref=old_keys, send_sem=sems.at[2], recv_sem=sems.at[3],
        device_id=at.attender(at.after(), at.c, at.a), device_id_type=MESH,
    )
    hand_on.start()
    total[...] = jnp.zeros_like(total)

    @pl.when(at.y != at.g)
    def _():
        wait_bytes(ends, sems.at[1])

    hand_on.wait_recv()

    def hand_back(first):
        done = pl.ds(first, TILE)
        back_halo[done, :] = total[done, :].astype(BF16)
        pltpu.make_async_remote_copy(
            src_ref=back_halo.at[done, :], dst_ref=halo_grad.at[done, :], send_sem=sems.at[16],
            recv_sem=sems.at[17], device_id=at.attender(at.before(), at.c, at.a),
            device_id_type=MESH,
        ).start()

    for p in range(2):
        wait_bytes(recv.at[:, columns[p]], sems.at[4 + p])
        attention(at, p, recv, keys, total, back, ends, hand_back if p else lambda first: None)
        put_back(p)
    wait_bytes(halo_grad, sems.at[17])
    back[:, 4 * PAIR :] = (total[pl.ds(BLOCK, BLOCK), :] + halo_grad[...].astype(F32)).astype(BF16)
    put_back(2)

    normed_grad = jnp.zeros((rows, deep), F32)
    attended, slopes = [[] for _ in range(2)], [[] for _ in range(HEADS_KV)]
    for p in range(2):
        wait_bytes(ret.at[:, :, columns[p]], sems.at[7 + p])
        for c in range(HEADS_KV):
            mine = dot_tn(permute, ret[c, :, 2 * PAIR * p : 2 * PAIR * (p + 1)])
            even, odd = mine[:, :PAIR], mine[:, PAIR:]
            slopes[c].append(jnp.where(low, even, swap_halves(odd)).astype(BF16))
            attended[p].append(jnp.where(low, swap_halves(even), odd).astype(BF16))
    both = jnp.concatenate([attended[p][c] for c in range(HEADS_KV) for p in range(2)], axis=1)
    loads[2].wait()
    for j in range(HEADS_KV):
        for h in range(2):
            first = 512 * j + 256 * h
            mixed = dot(both, out_half(j, h))
            restored_ref[:, first : first + 256] = (
                uout_ref[:, first : first + 256].astype(F32) - mixed
            ).astype(BF16)
    store = pltpu.make_async_copy(restored_ref, restored_hbm, local_sems.at[4])
    store.start()
    wait_bytes(ret.at[:, :, columns[2]], sems.at[9])
    for c in range(HEADS_KV):
        slopes[c].append(dot_tn(permute, ret[c, :, 4 * PAIR :]).astype(BF16))
        normed_grad = normed_grad + dot_nt(
            jnp.concatenate(slopes[c], axis=1),
            full[c, :, :, :, :QKV_COLS].reshape(deep, QKV_COLS),
        )
    loads[3].wait()
    low_f = lower_ref[...].astype(F32)
    inv = lax.rsqrt(jnp.mean(low_f * low_f, axis=1, keepdims=True) + 1e-05)
    unit = low_f * inv
    unit_grad = normed_grad * gain_ref[...]
    term = inv * (unit_grad - unit * jnp.mean(unit_grad * unit, axis=1, keepdims=True))
    backg_ref[...] = (lgrad_ref[...].astype(F32) + term).astype(BF16)
    store_last = pltpu.make_async_copy(backg_ref, backg_hbm, local_sems.at[5])
    store_last.start()

    gather.drain()
    hand_on.wait_send()
    wait_bytes(back_halo, sems.at[16])
    for part in range(3):
        for base in (10, 13):
            wait_bytes(recv.at[pl.ds(0, 31 * PIECE), columns[part]], sems.at[base + part])

    @pl.when(at.y == at.g)
    def _():
        wait_bytes(halo_grad.at[pl.ds(0, 448), :], sems.at[0])

    store.wait()
    store_last.wait()


def per_device(
    upper_out, lower_out, upper_grad, lower_grad, norm_gain, query_weight, key_weight,
    value_matrix, out_weight, route_table, doc_lengths,
):
    rows, width = lower_out.shape
    docs = doc_lengths.shape[1]
    vmem = pl.BlockSpec(memory_space=pltpu.VMEM)
    smem = pl.BlockSpec(memory_space=pltpu.SMEM)
    anywhere = pl.BlockSpec(memory_space=pl.ANY)
    dma = pltpu.SemaphoreType.DMA
    row_block = pltpu.VMEM((rows, width), BF16)
    return pl.pallas_call(
        kernel,
        out_shape=(jax.ShapeDtypeStruct((rows, width), BF16),) * 2,
        in_specs=[anywhere] * 4 + [vmem] * 5 + [smem] * 2,
        out_specs=(anywhere, anywhere),
        scratch_shapes=[row_block] * 6 + [
            pltpu.VMEM((HEADS_KV, RING, RING, 32, GROUP_COLS), BF16),
            row_block,
            pltpu.VMEM((HEADS_KV, rows, GROUP_COLS), BF16),
            pltpu.VMEM((BLOCK, GROUP_COLS), BF16),
            pltpu.VMEM((2 * BLOCK, PAIR), BF16),
            pltpu.VMEM((2 * BLOCK, PAIR), F32),
            pltpu.VMEM((BLOCK, GROUP_COLS), BF16),
            pltpu.VMEM((BLOCK, PAIR), BF16),
            pltpu.VMEM((BLOCK, PAIR), BF16),
            pltpu.VMEM((HEADS_KV, rows, GROUP_COLS), BF16),
            pltpu.VMEM((docs, TILE), jnp.int32),
            pltpu.VMEM((docs, TILE), jnp.int32),
            dma((2, 2, 4)), dma((2, 2, RING, 4)), dma((2, 14)), dma((8,)), dma((18,)), dma((6,)),
        ],
        compiler_params=pltpu.CompilerParams(
            collective_id=0, has_side_effects=True, vmem_limit_bytes=56 * 1024 * 1024
        ),
        name="coupling",
    )(
        lower_out, upper_grad, upper_out, lower_grad, norm_gain.reshape(1, width), query_weight,
        key_weight, value_matrix, out_weight, route_table, doc_lengths,
    )


def solution(mesh):
    rows = P(("grp", "sp"), None)
    return jax.shard_map(
        per_device,
        mesh=mesh,
        in_specs=(
            rows, rows, rows, rows, P(), P("sp", None), P("sp", None), P("sp", None),
            P("sp", None), P("grp", "sp", None), P("grp", None),
        ),
        out_specs=(rows, rows),
        check_vma=False,
    )
```

time: 130 us -> 108 us (0.83)
  Pallas kernels: 121 us -> 104 us
  local copies, waits for them, and re-layouts: 5.9 us -> 2.74 us
  other arithmetic: 1.5 us -> 0 us
    pallas_call x1, Pallas kernels: 121 us -> 104 us  [per_device(): pl.pallas_call(kernel, out_shape=(jax.ShapeDtypeStruct((rows, width), BF1...]
    unnamed x16 -> x4, local copies, waits for them, and re-layouts: 4.91 us -> 2.74 us
where the time goes in v2:
time: 108 us
  Pallas kernels  104 us (96%)
  local copies, waits for them, and re-layouts  2.74 us (3%)
    pallas_call x1, Pallas kernels, per_device(): pl.pallas_call(kernel, out_shape=(jax.ShapeDtypeStruct((rows, width), BF1...  104 us
    unnamed x4, local copies, waits for them, and re-layouts  2.74 us

profile of v2, /device:TPU:1, one launch (start us, length us, event | category | flops | bytes accessed | tf_op | source)
XLA Modules:
  0.0 107.6 jit_solution(6549156304633812026)
XLA Ops:
  0.6 104.2 %coupling.1 = (bf16[128,2048]{1,0:T(8,128)(2,1)}, bf16[128,2048]{1,0:T(8,128)(2,1)}) custom-call(bf16[128,2048]{1,0:T(8,128)(2,1)} %lower_hbm.1, bf16[128,2048]{1,0:T(8,128)(2,1)} %ugrad_hbm.1, bf16[128,2048]{1,0:T(8,128)(2,1)} %uout_hbm.1, bf16[128,2048]{1,0:T(8,128)(2,1)} %lgrad_hbm.1, f32[1,2048]{1,0:T(1,128)} %bitcast.1, bf16[32,1024]{1,0:T(8,128)(2,1)} %wq_ref.1, ...), custom_call_target="tpu_custom_call" | custom-call | tf_op jit(solution)/shard_map/coupling/pallas_call | solution.py:505
  104.9 0.0 copy-start
  104.9 1.9 %copy.15 = bf16[128,2048]{1,0:T(8,128)(2,1)} copy(bf16[128,2048]{1,0:T(8,128)(2,1)} %get-tuple-element.4) | data formatting | bytes 1048576
  106.8 0.0 copy-done
  106.8 0.8 copy.16
Async XLA Ops:
  104.9 2.0 %copy-start = (bf16[128,2048]{1,0:T(8,128)(2,1)S(1)}, bf16[128,2048]{1,0:T(8,128)(2,1)}, u32[]{:S(2)}) copy-start(bf16[128,2048]{1,0:T(8,128)(2,1)} %get-tuple-element.5) | copy-start | bytes 1572868

commit v3 on v2

v3 whole, which is shorter than its diff:
```python
import functools

import jax
import jax.numpy as jnp
from jax import lax
from jax.experimental import pallas as pl
from jax.experimental.pallas import tpu as pltpu
from jax.sharding import PartitionSpec as P

HEAD = 64
PAIR = 2 * HEAD
PIECE = 16
BLOCK = 512
TILE = 128
WINDOW = BLOCK + TILE
RING = 8
HEADS_KV = 4
GROUP_COLS = 4 * PAIR + PAIR
MESH = pl.DeviceIdType.MESH
F32 = jnp.float32
BF16 = jnp.bfloat16


def dot(a, b):
    return jnp.dot(a, b, preferred_element_type=F32)


def dot_nt(a, b):
    return lax.dot_general(a, b, (((1,), (1,)), ((), ())), preferred_element_type=F32)


def dot_tn(a, b):
    return lax.dot_general(a, b, (((0,), (0,)), ((), ())), preferred_element_type=F32)


def div(a, n):
    return lax.div(a, jnp.int32(n))


def mod(a, n):
    return lax.rem(a, jnp.int32(n))


class Place:
    def __init__(self):
        self.g = lax.axis_index("grp")
        self.s = lax.axis_index("sp")
        self.x, self.core = div(self.g, 2), mod(self.g, 2)
        self.z, self.y = div(self.s, RING), mod(self.s, RING)
        self.zp, self.zb = div(self.z, 2), mod(self.z, 2)
        self.block = self.x * 4 + self.zp
        self.a = self.y
        self.c = self.core + 2 * self.zb
        self.mine = self.c * 8 + self.a
        self.source = self.zb * 16 + self.y * 2 + self.core

    def attender(self, block, c, a):
        return {
            "grp": div(block, 4) * 2 + mod(c, 2),
            "sp": (mod(block, 4) * 2 + div(c, 2)) * RING + a,
        }

    def home(self, block, source):
        return {
            "grp": div(block, 4) * 2 + mod(source, 2),
            "sp": (mod(block, 4) * 2 + div(source, 16)) * RING + mod(div(source, 2), RING),
        }

    def after(self):
        return mod(self.block + 1, 16)

    def before(self):
        return mod(self.block + 15, 16)


def greet(at):
    barrier = pltpu.get_barrier_semaphore()

    def signal(device):
        pl.semaphore_signal(barrier, inc=1, device_id=device, device_id_type=MESH)

    for dz in (1, 2, RING - 2, RING - 1):
        signal({"grp": at.g, "sp": mod(at.z + dz, RING) * RING + at.y})
    signal(at.attender(at.after(), at.c, at.a))
    signal(at.attender(at.before(), at.c, at.a))

    def column(d, carry):
        signal({"grp": mod(at.g + d, 8), "sp": at.s})
        return carry

    def own(d, carry):
        other = mod(at.mine + d, 32)
        signal(at.attender(at.block, div(other, 8), mod(other, 8)))
        return carry

    lax.fori_loop(1, 8, column, 0)
    lax.fori_loop(1, 32, own, 0)
    pl.semaphore_wait(barrier, 4 + 2 + 7 + 31)


def wait_bytes(ref, sem):
    pltpu.make_async_copy(ref, ref, sem).wait()


class Gather:
    def __init__(self, at, full, rest, sems):
        self.at, self.full, self.rest = at, full, rest
        self.first_in, self.second_in, self.share_in, self.cross_in, self.cross_share_in, self.out = sems
        along_y = [mod(at.y + k, RING) for k in range(RING)]
        along_z = [mod(at.z + k, RING) for k in range(RING)]
        self.places = ((along_y, along_z), (along_z, along_y))
        self.crossing = []

    def shard(self, order, core, i1, i2, half):
        z, y = (i2, i1) if order == 0 else (i1, i2)
        units = slice(None) if half is None else (pl.ds(0, 4), pl.ds(4, 3))[half]
        return self.full.at[2 * core + order, z, y, units]

    def line(self, order, core, d):
        j = 2 * core + order
        i2 = self.places[order][1][d]
        return self.full.at[j, i2] if order == 0 else self.full.at[j, :, i2]

    def rest_line(self, order, core, d, slots):
        return self.rest.at[2 * core + order, slots, self.places[order][1][d]]

    def step(self, order, axis, way):
        at = self.at
        if (order + axis) % 2 == 0:
            return {"grp": at.g, "sp": at.z * RING + self.places[0][0][way % RING]}
        return {"grp": at.g, "sp": self.places[0][1][way % RING] * RING + at.y}

    def first(self, order, way, t, arriving):
        half = None if t < 4 else (1 - way) // 2
        hops = 1 if t % 2 else 2
        back = t if arriving else t - hops
        i1 = self.places[order][0][(-way * back) % RING]
        block = self.shard(order, self.at.core, i1, self.places[order][1][0], half)
        return pltpu.make_async_remote_copy(
            src_ref=block, dst_ref=block, send_sem=self.out.at[order],
            recv_sem=self.first_in.at[order, (1 - way) // 2, t - 1],
            device_id=self.step(order, 0, way * hops), device_id_type=MESH,
        )

    def second(self, order, way, k, m, i2):
        half = None if m < 4 else (1 - way) // 2
        i1 = self.places[order][0][k % RING]
        block = self.shard(order, self.at.core, i1, i2, half)
        return pltpu.make_async_remote_copy(
            src_ref=block, dst_ref=block, send_sem=self.out.at[2 + order],
            recv_sem=self.second_in.at[order, (1 - way) // 2, (k + RING) % RING, m - 1],
            device_id=self.step(order, 1, way), device_id_type=MESH,
        )

    def share_block(self, order, core, n):
        if n < 7:
            first, second = self.places[order]
            return self.shard(order, core, first[n + 1], second[0], None)
        return self.line(order, core, n - 6)

    def to_sibling(self, block, send_sem, recv_sem):
        at = self.at
        pltpu.make_async_remote_copy(
            src_ref=block, dst_ref=block, send_sem=send_sem, recv_sem=recv_sem,
            device_id={"grp": at.x * 2 + 1 - at.core, "sp": at.s}, device_id_type=MESH,
        ).start()

    def hand_over(self, order, n):
        self.to_sibling(
            self.share_block(order, self.at.core, n),
            self.out.at[4 + (n >= 7) * 2 + order], self.share_in.at[order, n],
        )

    def cross(self, order, d, source, target, way):
        at = self.at
        return pltpu.make_async_remote_copy(
            src_ref=self.rest_line(order, at.core, d, source),
            dst_ref=self.rest_line(order, at.core, d, target),
            send_sem=self.out.at[8 + order], recv_sem=self.cross_in.at[order, d, target - 1],
            device_id={"grp": mod(at.x + way + 4, 4) * 2 + at.core, "sp": at.s},
            device_id_type=MESH,
        )

    def start_cross(self, order, d):
        j = 2 * self.at.core + order
        i2 = self.places[order][1][d]
        if order == 0:
            self.rest[j, 0, i2] = self.full[j, i2, :, 6]
        else:
            self.rest[j, 0, i2] = self.full[j, :, i2, 6]
        self.cross(order, d, 0, 3, 1).start()
        self.cross(order, d, 0, 1, -1).start()
        self.crossing.append((order, d))

    def forward_cross(self, items):
        for order, d in items:
            self.cross(order, d, 0, 3, 1).wait_recv()
            self.cross(order, d, 0, 1, -1).wait_recv()
            if d % 2 == 0:
                self.cross(order, d, 3, 2, 1).start()
            else:
                self.cross(order, d, 1, 2, -1).start()

    def share_cross(self, items):
        for order, d in items:
            self.cross(order, d, 3, 2, 1).wait_recv()
            self.to_sibling(
                self.rest_line(order, self.at.core, d, pl.ds(1, 3)),
                self.out.at[10 + order], self.cross_share_in.at[order, d],
            )

    def run(self, filler):
        for tick in range(7):
            for order in (0, 1):
                for way in (1, -1):
                    for t in {1: (1, 2), 2: (3, 4)}.get(tick, ()):
                        self.first(order, way, t, True).wait_recv()
                        if t < 4:
                            self.hand_over(order, (-way * t) % RING - 1)
                    for t in {0: (1, 2), 1: (3, 4)}.get(tick, ()):
                        self.first(order, way, t, False).start()
                if tick == 2:
                    self.hand_over(order, 3)
                    self.start_cross(order, 0)
            for k in (3, -3, 4, 2, -2, 1, -1, 0):
                m = tick - (abs(k) + 1) // 2 + 1
                if m < 1 or m > 5:
                    continue
                for order in (0, 1):
                    for way in (1, -1):
                        i2 = self.places[order][1][(-way * (m - 1)) % RING]
                        if m > 1:
                            self.second(order, way, k, m - 1, i2).wait_recv()
                        if m < 5:
                            self.second(order, way, k, m, i2).start()
                        if k == 4 and 1 < m < 5:
                            d = (-way * (m - 1)) % RING
                            self.hand_over(order, 6 + d)
                            self.start_cross(order, d)
                    if k == 4 and m == 5:
                        self.hand_over(order, 10)
                        self.start_cross(order, 4)
                next(filler, None)
        for _ in filler:
            pass
        self.forward_cross(self.crossing[:10])
        for order in (0, 1):
            for n in range(14):
                wait_bytes(
                    self.share_block(order, 1 - self.at.core, n), self.share_in.at[order, n]
                )

    def finish_cross(self):
        self.share_cross(self.crossing)
        for order in (0, 1):
            for d in range(RING):
                wait_bytes(
                    self.rest_line(order, 1 - self.at.core, d, pl.ds(1, 3)),
                    self.cross_share_in.at[order, d],
                )

    def drain(self):
        seven = self.full.at[0, 0, pl.ds(0, 7)]
        lines = self.full.at[0, pl.ds(0, 7)]
        rest = self.rest.at[0, pl.ds(0, 3)]
        for order in (0, 1):
            for n, ref in enumerate((seven, lines, seven, lines, rest, rest)):
                wait_bytes(ref, self.out.at[2 * n + order])


def swap_halves(a):
    return pltpu.roll(a, HEAD, 1)


def two_heads(pair, scale):
    low = lax.broadcasted_iota(jnp.int32, (1, PAIR), 1) < HEAD
    first = jnp.where(low, scale, 0.0).astype(BF16)
    second = jnp.where(low, 0.0, scale).astype(BF16)
    return jnp.concatenate([pair * first, pair * second], axis=0)


def stacked(a):
    return jnp.concatenate([a[:, :TILE], a[:, TILE:]], axis=0)


def attend(at, pair, recv, keys_twice, keys_t, probs, outs, back, ends_ref):
    ends = ends_ref[...]

    def tile(t, carry):
        first = pl.multiple_of(t * TILE, TILE)
        window = pl.ds(first, WINDOW)
        queries = two_heads(recv[pl.ds(first, TILE), PAIR * pair : PAIR * (pair + 1)], 0.125)
        scores = dot_nt(keys_twice[window, :], queries)
        position = at.block * BLOCK + first + lax.broadcasted_iota(jnp.int32, (1, TILE), 1)
        began = jnp.max(jnp.where(ends <= position, ends, 0), axis=0, keepdims=True)
        key_position = (at.block - 1) * BLOCK + first + lax.broadcasted_iota(
            jnp.int32, (WINDOW, TILE), 0
        )
        allowed = (key_position >= began) & (key_position <= position)
        halves = []
        for i in range(2):
            cols = slice(TILE * i, TILE * (i + 1))
            s = jnp.where(allowed, scores[:, cols], -jnp.inf)
            raised = jnp.exp(s - jnp.max(s, axis=0, keepdims=True))
            prob = raised * (1.0 / jnp.sum(raised, axis=0, keepdims=True))
            probs[pair, t, :, cols] = prob
            halves.append(prob.astype(BF16))
        out = stacked(dot(keys_t[HEAD:, window], jnp.concatenate(halves, axis=1)))
        out = out.astype(BF16).astype(F32)
        outs[pair, t] = out
        back[pl.ds(first, TILE), 2 * PAIR * pair : 2 * PAIR * pair + PAIR] = out.T.astype(BF16)
        return carry

    lax.fori_loop(0, BLOCK // TILE, tile, 0)


def differentiate(
    pair, recv, values_twice, keys_t, probs, outs, key_total, value_total, back, finish
):
    def tile(t, carry):
        first = pl.multiple_of(t * TILE, TILE)
        window = pl.ds(first, WINDOW)
        mine = pl.ds(first, TILE)
        queries = two_heads(recv[mine, PAIR * pair : PAIR * (pair + 1)], 0.125)
        grad = recv[mine, 2 * PAIR + PAIR * pair : 2 * PAIR + PAIR * (pair + 1)]
        grads = two_heads(grad, 1.0)
        prob_grad = dot_nt(values_twice[window, :], grads)
        product = grad.astype(F32).T * outs[pair, t]
        halves, slopes = [], []
        for i in range(2):
            cols = slice(TILE * i, TILE * (i + 1))
            delta = jnp.sum(product[HEAD * i : HEAD * (i + 1), :], axis=0, keepdims=True)
            prob = probs[pair, t, :, cols]
            halves.append(prob.astype(BF16))
            slopes.append((prob * (prob_grad[:, cols] - delta)).astype(BF16))
        slope = jnp.concatenate(slopes, axis=1)
        query_grad = stacked(dot(keys_t[:HEAD, window], slope)) * 0.125
        back[mine, 2 * PAIR * pair + PAIR : 2 * PAIR * (pair + 1)] = query_grad.T.astype(BF16)
        key_total[window, :] += dot(slope, queries)
        value_total[window, :] += dot(jnp.concatenate(halves, axis=1), grads)
        finish(first)
        return carry

    lax.fori_loop(0, BLOCK // TILE, tile, 0)


def kernel(
    lower_hbm, ugrad_hbm, uout_hbm, lgrad_hbm, gain_ref, wq_ref, wk_ref, wv_ref, wo_ref,
    route_ref, lens_ref,
    restored_hbm, backg_hbm,
    lower_ref, ugrad_ref, uout_ref, lgrad_ref, restored_ref, backg_ref,
    full, rest, normed, send, recv, keys, keys_twice, values_twice, keys_t, probs, outs,
    key_total, value_total, back, back_halo, halo_grad, ret, ends_own, ends,
    first_in, second_in, share_in, cross_in, cross_share_in, gather_out, sems, local_sems,
):
    at = Place()
    rows, width = lower_ref.shape
    deep = RING * RING * 32
    query_cols = HEADS_KV * 4 * HEAD
    loads = [
        pltpu.make_async_copy(src, dst, local_sems.at[n])
        for n, (src, dst) in enumerate(
            ((lower_hbm, lower_ref), (ugrad_hbm, ugrad_ref), (uout_hbm, uout_ref),
             (lgrad_hbm, lgrad_ref))
        )
    ]
    for load in loads:
        load.start()

    low_w = lax.broadcasted_iota(jnp.int32, (32, PAIR), 1) < HEAD
    for j in range(HEADS_KV):
        k2 = wk_ref[:, PAIR * (j // 2) : PAIR * (j // 2 + 1)].astype(F32)
        v2 = wv_ref[:, PAIR * (j // 2) : PAIR * (j // 2 + 1)].astype(F32)
        if j % 2 == 0:
            kv = jnp.where(low_w, k2, swap_halves(v2))
        else:
            kv = jnp.where(low_w, swap_halves(k2), v2)
        tiles = [wq_ref[:, 256 * j + PAIR * t : 256 * j + PAIR * (t + 1)] for t in range(2)]
        for t, tile in enumerate(tiles + [kv.astype(BF16)]):
            for h in range(2):
                full[j, at.z, at.y, 2 * t + h] = tile[PIECE * h : PIECE * (h + 1), :]
        own = pl.multiple_of(512 * j + PAIR * at.x, PAIR)
        full[j, at.z, at.y, 6] = wo_ref[:, pl.ds(own, PAIR)]
    docs = ends.shape[0]
    doc = lax.broadcasted_iota(jnp.int32, (docs, TILE), 0)
    until = jnp.zeros((docs, TILE), jnp.int32)
    so_far = 0
    for k in range(docs):
        so_far = so_far + lens_ref[0, k]
        until = jnp.where(doc == k, so_far, until)
    ends_own[...] = until
    greet(at)

    @pl.when(at.y == at.g)
    def _():
        def tell(d, carry):
            pltpu.make_async_remote_copy(
                src_ref=ends_own, dst_ref=ends, send_sem=sems.at[0], recv_sem=sems.at[1],
                device_id={"grp": mod(at.g + d, 8), "sp": at.s}, device_id_type=MESH,
            ).start()
            return carry

        lax.fori_loop(1, 8, tell, 0)
        ends[...] = ends_own[...]

    def norm():
        loads[0].wait()
        for r in range(0, rows, PIECE):
            part = lower_ref[r : r + PIECE, :].astype(F32)
            inv = lax.rsqrt(jnp.mean(part * part, axis=1, keepdims=True) + 1e-05)
            normed[r : r + PIECE, :] = ((part * inv) * gain_ref[...]).astype(BF16)
            yield

    gather = Gather(
        at, full, rest, (first_in, second_in, share_in, cross_in, cross_share_in, gather_out)
    )
    gather.run(norm())

    def in_weights(c, tiles=(0, 1, 2)):
        return jnp.concatenate(
            [full[c, :, :, 2 * t : 2 * t + 2].reshape(deep, PAIR) for t in tiles], axis=1
        )

    def out_columns(j, u):
        return pl.ds(pl.multiple_of(512 * j + PAIR * (mod(at.x + u, 4)), PAIR), PAIR)

    def out_weights(j, h):
        parts = []
        for u in (2 * h, 2 * h + 1):
            if u == 0:
                part = full[j, :, :, 6]
            elif j % 2 == 0:
                part = rest[j, u]
            else:
                part = jnp.concatenate([rest[j, u, :, z] for z in range(RING)], axis=0)
            parts.append(part.reshape(query_cols, PAIR))
        return jnp.concatenate(parts, axis=1)

    def piece(i):
        return pl.ds(pl.multiple_of(i * PIECE, PIECE), PIECE)

    columns = (pl.ds(0, 2 * PAIR), pl.ds(2 * PAIR, 2 * PAIR), pl.ds(4 * PAIR, PAIR))

    def put_out(part):
        cols = columns[part]

        def target(source):
            if part == 2:
                return keys.at[pl.ds(pl.multiple_of(BLOCK + source * PIECE, PIECE), PIECE), :]
            return recv.at[piece(source), cols]

        pltpu.make_async_copy(
            send.at[at.c, piece(at.a), cols], target(at.source), sems.at[4 + part]
        ).start()

        def one(d):
            other = mod(at.mine + d, 32)
            c, a = div(other, 8), mod(other, 8)
            pltpu.make_async_remote_copy(
                src_ref=send.at[c, piece(a), cols], dst_ref=target(at.source),
                send_sem=sems.at[10 + part], recv_sem=sems.at[4 + part],
                device_id=at.attender(at.block, c, a), device_id_type=MESH,
            ).start()

        for d in range(1, 32):
            one(d)

    def put_back(part):
        cols = columns[part]
        pltpu.make_async_copy(
            back.at[piece(at.source), cols], ret.at[at.c, piece(at.a), cols], sems.at[7 + part]
        ).start()

        def one(d):
            source = mod(at.source + d, 32)
            pltpu.make_async_remote_copy(
                src_ref=back.at[piece(source), cols], dst_ref=ret.at[at.c, piece(at.a), cols],
                send_sem=sems.at[13 + part], recv_sem=sems.at[7 + part],
                device_id=at.home(at.block, source), device_id_type=MESH,
            ).start()

        for d in range(1, 32):
            one(d)

    row = lax.broadcasted_iota(jnp.int32, (1, rows), 1)
    dest = row % PIECE
    for p in range(rows // PIECE):
        dest = jnp.where(row // PIECE == p, dest + route_ref[0, 0, p] * PIECE, dest)
    permute = (
        lax.broadcasted_iota(jnp.int32, (rows, rows), 0) == dest
    ).astype(F32).astype(BF16)

    for c in range(HEADS_KV):
        if c == 2:
            gather.forward_cross(gather.crossing[10:])
        qkv = dot(normed[...], in_weights(c)).astype(BF16)
        qkv = dot(permute, qkv).astype(BF16)
        send[c, :, : 4 * HEAD] = qkv[:, : 4 * HEAD]
        send[c, :, 8 * HEAD :] = qkv[:, 4 * HEAD :]
    put_out(2)
    put_out(0)
    gather.finish_cross()

    own_keys, old_keys = keys.at[pl.ds(BLOCK, BLOCK), :], keys.at[pl.ds(0, BLOCK), :]
    wait_bytes(own_keys, sems.at[6])
    hand_on = pltpu.make_async_remote_copy(
        src_ref=own_keys, dst_ref=old_keys, send_sem=sems.at[2], recv_sem=sems.at[3],
        device_id=at.attender(at.after(), at.c, at.a), device_id_type=MESH,
    )
    hand_on.start()
    loads[1].wait()
    grad_cols = jnp.zeros((rows, query_cols), F32)
    for j in range(HEADS_KV):
        for h in range(2):
            above = jnp.concatenate(
                [ugrad_ref[:, out_columns(j, u)] for u in (2 * h, 2 * h + 1)], axis=1
            )
            grad_cols = grad_cols + dot_nt(above, out_weights(j, h))
    grad_cols = dot(permute, grad_cols.astype(BF16)).astype(BF16)
    for c in range(HEADS_KV):
        send[c, :, 4 * HEAD : 8 * HEAD] = grad_cols[:, 4 * HEAD * c : 4 * HEAD * (c + 1)]
    put_out(1)
    key_total[...] = jnp.zeros_like(key_total)
    value_total[...] = jnp.zeros_like(value_total)

    @pl.when(at.y != at.g)
    def _():
        wait_bytes(ends, sems.at[1])

    hand_on.wait_recv()
    here = keys[...].astype(F32)
    there = swap_halves(here)
    low_keys = lax.broadcasted_iota(jnp.int32, (2 * BLOCK, PAIR), 1) < HEAD
    keys_twice[...] = jnp.where(low_keys, here, there).astype(BF16)
    values_twice[...] = jnp.where(low_keys, there, here).astype(BF16)
    keys_t[...] = here.T.astype(BF16)

    def key_value_grads(span):
        k, v = key_total[span, :], value_total[span, :]
        low_span = lax.broadcasted_iota(jnp.int32, k.shape, 1) < HEAD
        return jnp.where(low_span, k + swap_halves(k), v + swap_halves(v))

    def hand_back(first):
        done = pl.ds(first, TILE)
        back_halo[done, :] = key_value_grads(done).astype(BF16)
        pltpu.make_async_remote_copy(
            src_ref=back_halo.at[done, :], dst_ref=halo_grad.at[done, :], send_sem=sems.at[16],
            recv_sem=sems.at[17], device_id=at.attender(at.before(), at.c, at.a),
            device_id_type=MESH,
        ).start()

    wait_bytes(recv.at[:, columns[0]], sems.at[4])
    for p in range(2):
        attend(at, p, recv, keys_twice, keys_t, probs, outs, back, ends)
    wait_bytes(recv.at[:, columns[1]], sems.at[5])
    for p in range(2):
        differentiate(
            p, recv, values_twice, keys_t, probs, outs, key_total, value_total, back,
            hand_back if p else lambda first: None,
        )
        put_back(p)
    wait_bytes(halo_grad, sems.at[17])
    back[:, 4 * PAIR :] = (
        key_value_grads(pl.ds(BLOCK, BLOCK)) + halo_grad[...].astype(F32)
    ).astype(BF16)
    put_back(2)

    normed_grad = jnp.zeros((rows, deep), F32)
    attended, slopes = [[] for _ in range(2)], [[] for _ in range(HEADS_KV)]
    for p in range(2):
        wait_bytes(ret.at[:, :, columns[p]], sems.at[7 + p])
        for c in range(HEADS_KV):
            mine = dot_tn(permute, ret[c, :, 2 * PAIR * p : 2 * PAIR * (p + 1)]).astype(BF16)
            attended[p].append(mine[:, :PAIR])
            slopes[c].append(mine[:, PAIR:])
    both = jnp.concatenate([attended[p][c] for c in range(HEADS_KV) for p in range(2)], axis=1)
    loads[2].wait()
    for j in range(HEADS_KV):
        for h in range(2):
            mixed = dot(both, out_weights(j, h))
            for i in range(2):
                cols = out_columns(j, 2 * h + i)
                restored_ref[:, cols] = (
                    uout_ref[:, cols].astype(F32) - mixed[:, PAIR * i : PAIR * (i + 1)]
                ).astype(BF16)
    store = pltpu.make_async_copy(restored_ref, restored_hbm, local_sems.at[4])
    store.start()
    for c in range(HEADS_KV):
        normed_grad = normed_grad + dot_nt(
            jnp.concatenate(slopes[c], axis=1), in_weights(c, (0, 1))
        )
    low_f = lower_ref[...].astype(F32)
    inv = lax.rsqrt(jnp.mean(low_f * low_f, axis=1, keepdims=True) + 1e-05)
    unit = low_f * inv
    loads[3].wait()
    wait_bytes(ret.at[:, :, columns[2]], sems.at[9])
    for c in range(0, HEADS_KV, 2):
        both = jnp.concatenate([ret[c, :, 4 * PAIR :], ret[c + 1, :, 4 * PAIR :]], axis=1)
        both = dot_tn(permute, both).astype(BF16)
        weights = jnp.concatenate([in_weights(c, (2,)), in_weights(c + 1, (2,))], axis=1)
        normed_grad = normed_grad + dot_nt(both, weights)
    unit_grad = normed_grad * gain_ref[...]
    term = inv * (unit_grad - unit * jnp.mean(unit_grad * unit, axis=1, keepdims=True))
    backg_ref[...] = (lgrad_ref[...].astype(F32) + term).astype(BF16)
    store_last = pltpu.make_async_copy(backg_ref, backg_hbm, local_sems.at[5])
    store_last.start()

    gather.drain()
    hand_on.wait_send()
    wait_bytes(back_halo, sems.at[16])
    for part in range(3):
        for base in (10, 13):
            wait_bytes(recv.at[pl.ds(0, 31 * PIECE), columns[part]], sems.at[base + part])

    @pl.when(at.y == at.g)
    def _():
        wait_bytes(halo_grad.at[pl.ds(0, 448), :], sems.at[0])

    store.wait()
    store_last.wait()


def per_device(
    upper_out, lower_out, upper_grad, lower_grad, norm_gain, query_weight, key_weight,
    value_matrix, out_weight, route_table, doc_lengths,
):
    rows, width = lower_out.shape
    docs = doc_lengths.shape[1]
    vmem = pl.BlockSpec(memory_space=pltpu.VMEM)
    smem = pl.BlockSpec(memory_space=pltpu.SMEM)
    anywhere = pl.BlockSpec(memory_space=pl.ANY)
    dma = pltpu.SemaphoreType.DMA
    row_block = pltpu.VMEM((rows, width), BF16)
    return pl.pallas_call(
        kernel,
        out_shape=(jax.ShapeDtypeStruct((rows, width), BF16),) * 2,
        in_specs=[anywhere] * 4 + [vmem] * 5 + [smem] * 2,
        out_specs=(anywhere, anywhere),
        scratch_shapes=[row_block] * 6 + [
            pltpu.VMEM((HEADS_KV, RING, RING, 7, PIECE, PAIR), BF16),
            pltpu.VMEM((HEADS_KV, 4, RING, RING, PIECE, PAIR), BF16),
            row_block,
            pltpu.VMEM((HEADS_KV, rows, GROUP_COLS), BF16),
            pltpu.VMEM((BLOCK, GROUP_COLS), BF16),
            pltpu.VMEM((2 * BLOCK, PAIR), BF16),
            pltpu.VMEM((2 * BLOCK, PAIR), BF16),
            pltpu.VMEM((2 * BLOCK, PAIR), BF16),
            pltpu.VMEM((PAIR, 2 * BLOCK), BF16),
            pltpu.VMEM((2, BLOCK // TILE, WINDOW, 2 * TILE), F32),
            pltpu.VMEM((2, BLOCK // TILE, PAIR, TILE), F32),
            pltpu.VMEM((2 * BLOCK, PAIR), F32),
            pltpu.VMEM((2 * BLOCK, PAIR), F32),
            pltpu.VMEM((BLOCK, GROUP_COLS), BF16),
            pltpu.VMEM((BLOCK, PAIR), BF16),
            pltpu.VMEM((BLOCK, PAIR), BF16),
            pltpu.VMEM((HEADS_KV, rows, GROUP_COLS), BF16),
            pltpu.VMEM((docs, TILE), jnp.int32),
            pltpu.VMEM((docs, TILE), jnp.int32),
            dma((2, 2, 4)), dma((2, 2, RING, 4)), dma((2, 14)), dma((2, RING, 3)), dma((2, RING)),
            dma((12,)), dma((18,)), dma((6,)),
        ],
        compiler_params=pltpu.CompilerParams(
            collective_id=0, has_side_effects=True, vmem_limit_bytes=56 * 1024 * 1024
        ),
        name="coupling",
    )(
        lower_out, upper_grad, upper_out, lower_grad, norm_gain.reshape(1, width), query_weight,
        key_weight, value_matrix, out_weight, route_table, doc_lengths,
    )


def solution(mesh):
    rows = P(("grp", "sp"), None)
    return jax.shard_map(
        per_device,
        mesh=mesh,
        in_specs=(
            rows, rows, rows, rows, P(), P("sp", None), P("sp", None), P("sp", None),
            P("sp", None), P("grp", "sp", None), P("grp", None),
        ),
        out_specs=(rows, rows),
        check_vma=False,
    )
```

time: 108 us -> 103 us (0.954)
  Pallas kernels: 104 us -> 99.8 us
    pallas_call x1, Pallas kernels: 104 us -> 99.8 us  [per_device(): pl.pallas_call(kernel, out_shape=(jax.ShapeDtypeStruct((rows, width), BF1...]
where the time goes in v3:
time: 103 us
  Pallas kernels  99.8 us (97%)
  local copies, waits for them, and re-layouts  2.74 us (3%)
    pallas_call x1, Pallas kernels, per_device(): pl.pallas_call(kernel, out_shape=(jax.ShapeDtypeStruct((rows, width), BF1...  99.8 us
    unnamed x4, local copies, waits for them, and re-layouts  2.74 us

profile of v3, /device:TPU:1, one launch (start us, length us, event | category | flops | bytes accessed | tf_op | source)
XLA Modules:
  0.0 103.2 jit_solution(16918927799876793188)
XLA Ops:
  0.6 99.8 %coupling.1 = (bf16[128,2048]{1,0:T(8,128)(2,1)}, bf16[128,2048]{1,0:T(8,128)(2,1)}) custom-call(bf16[128,2048]{1,0:T(8,128)(2,1)} %lower_hbm.1, bf16[128,2048]{1,0:T(8,128)(2,1)} %ugrad_hbm.1, bf16[128,2048]{1,0:T(8,128)(2,1)} %uout_hbm.1, bf16[128,2048]{1,0:T(8,128)(2,1)} %lgrad_hbm.1, f32[1,2048]{1,0:T(1,128)} %bitcast.1, bf16[32,1024]{1,0:T(8,128)(2,1)} %wq_ref.1, ...), custom_call_target="tpu_custom_call" | custom-call | tf_op jit(solution)/shard_map/coupling/pallas_call | solution.py:634
  100.4 0.0 copy-start
  100.5 1.9 %copy.15 = bf16[128,2048]{1,0:T(8,128)(2,1)} copy(bf16[128,2048]{1,0:T(8,128)(2,1)} %get-tuple-element.4) | data formatting | bytes 1048576
  102.4 0.0 copy-done
  102.4 0.8 copy.16
Async XLA Ops:
  100.4 2.0 %copy-start = (bf16[128,2048]{1,0:T(8,128)(2,1)S(1)}, bf16[128,2048]{1,0:T(8,128)(2,1)}, u32[]{:S(2)}) copy-start(bf16[128,2048]{1,0:T(8,128)(2,1)} %get-tuple-element.5) | copy-start | bytes 1572868

commit v4 on v3

--- a/solution.py
+++ b/solution.py
@@ -95,7 +95,7 @@
 
     lax.fori_loop(1, 8, column, 0)
     lax.fori_loop(1, 32, own, 0)
-    pl.semaphore_wait(barrier, 4 + 2 + 7 + 31)
+    return lambda: pl.semaphore_wait(barrier, 4 + 2 + 7 + 31)
 
 
 def wait_bytes(ref, sem):
@@ -366,6 +366,7 @@
     ]
     for load in loads:
         load.start()
+    greeted = greet(at)
 
     low_w = lax.broadcasted_iota(jnp.int32, (32, PAIR), 1) < HEAD
     for j in range(HEADS_KV):
@@ -389,7 +390,7 @@
         so_far = so_far + lens_ref[0, k]
         until = jnp.where(doc == k, so_far, until)
     ends_own[...] = until
-    greet(at)
+    greeted()
 
     @pl.when(at.y == at.g)
     def _():

time: 103 us -> 103 us (level)
  no operation moved by 1% of the time
where the time goes in v4:
time: 103 us
  Pallas kernels  99.8 us (97%)
  local copies, waits for them, and re-layouts  2.74 us (3%)
    pallas_call x1, Pallas kernels, per_device(): pl.pallas_call(kernel, out_shape=(jax.ShapeDtypeStruct((rows, width), BF1...  99.8 us
    unnamed x4, local copies, waits for them, and re-layouts  2.74 us

profile of v4, /device:TPU:1, one launch (start us, length us, event | category | flops | bytes accessed | tf_op | source)
XLA Modules:
  0.0 103.2 jit_solution(1762436763561698353)
XLA Ops:
  0.6 99.8 %coupling.1 = (bf16[128,2048]{1,0:T(8,128)(2,1)}, bf16[128,2048]{1,0:T(8,128)(2,1)}) custom-call(bf16[128,2048]{1,0:T(8,128)(2,1)} %lower_hbm.1, bf16[128,2048]{1,0:T(8,128)(2,1)} %ugrad_hbm.1, bf16[128,2048]{1,0:T(8,128)(2,1)} %uout_hbm.1, bf16[128,2048]{1,0:T(8,128)(2,1)} %lgrad_hbm.1, f32[1,2048]{1,0:T(1,128)} %bitcast.1, bf16[32,1024]{1,0:T(8,128)(2,1)} %wq_ref.1, ...), custom_call_target="tpu_custom_call" | custom-call | tf_op jit(solution)/shard_map/coupling/pallas_call | solution.py:635
  100.5 0.0 copy-start
  100.5 1.9 %copy.15 = bf16[128,2048]{1,0:T(8,128)(2,1)} copy(bf16[128,2048]{1,0:T(8,128)(2,1)} %get-tuple-element.4) | data formatting | bytes 1048576
  102.4 0.0 copy-done
  102.4 0.8 copy.16
Async XLA Ops:
  100.5 2.0 %copy-start = (bf16[128,2048]{1,0:T(8,128)(2,1)S(1)}, bf16[128,2048]{1,0:T(8,128)(2,1)}, u32[]{:S(2)}) copy-start(bf16[128,2048]{1,0:T(8,128)(2,1)} %get-tuple-element.5) | copy-start | bytes 1572868
